TPU v7x, 512 devices: a whole 4x8x8 slice. The times are simulated.
512 devices in a mesh: seq: 64 (over y, x, core), grp: 8 (over z).
Axes of the slice: x: 4, y: 8, z: 8, core: 2. Of those that a mesh axis runs over, the one named last changes fastest.
Arguments:
- query: bfloat16 [65536, 4096], P(('seq', 'grp')), may hold values from -64 to 64
- keys: bfloat16 [65536, 1024], P(('seq', 'grp')), may hold values from -4.5 to 4.5
- values: bfloat16 [65536, 1024], P(('seq', 'grp')), may hold values from -4.5 to 4.5
- output_cotangent: bfloat16 [65536, 4096], P(('seq', 'grp')), may hold values from -4.5 to 4.5
- select: int32 [512, 8, 8], P(None, 'grp'), may hold values from 0 to 511, as said below
Outputs:
- grad_query: bfloat16 [65536, 4096], P('seq', 'grp')
- key_gradient: bfloat16 [65536, 1024], P('seq', 'grp')
- value_gradient: bfloat16 [65536, 1024], P('seq', 'grp')
Inputs may be any that keep to these rules, and one draw needn't show every extreme that they name: select[b, c, 0] = b; the other 7 entries of a row are distinct blocks other than b, all earlier than b when b >= 7; for smaller b they are the b earlier blocks and some later ones.
All inputs are finite; a program needn't handle non-finite values.
Results may differ from a plain program's by a relative error of at most 0.019.
Values may be sent and summed in bfloat16 or wider, within the bound.
A program may use at most 128 MiB of HBM per device.

v0:
```python
import jax
import jax.numpy as jnp
from jax import lax
from jax.sharding import PartitionSpec as P

HEAD_SIZE = 128
QUERY_HEADS = 32
KEY_HEADS = 8
TOK_DEV = 128
BLOCK_TOKENS = 128
CHOSEN_BLOCKS = 8


def block_backward(q_rows, grad_rows, key_value_pairs, query_pos, key_positions, factor):
    head_width = q_rows.shape[-1]
    keys_part = key_value_pairs[..., :head_width]
    vals_part = key_value_pairs[..., head_width:]
    score_matrix = (
        jnp.einsum("tcgd,ckd->cgtk", q_rows, keys_part, preferred_element_type=jnp.float32) * factor
    )
    allowed = key_positions[:, None, None, :] <= query_pos[None, None, :, None]
    score_matrix = jnp.where(allowed, score_matrix, -jnp.inf)
    highest = jnp.max(score_matrix, axis=3, keepdims=True)
    weights = jnp.exp(score_matrix - highest)
    probability = weights / jnp.sum(weights, axis=3, keepdims=True)
    probs_low = probability.astype(jnp.bfloat16)
    recomputed = jnp.einsum(
        "cgtk,ckd->tcgd", probs_low, vals_part, preferred_element_type=jnp.float32
    )
    row_delta = jnp.sum(grad_rows.astype(jnp.float32) * recomputed, axis=3)
    row_delta = jnp.transpose(row_delta, (1, 2, 0))[..., None]
    dprobs = jnp.einsum("tcgd,ckd->cgtk", grad_rows, vals_part, preferred_element_type=jnp.float32)
    dscores = (probability * (dprobs - row_delta)).astype(jnp.bfloat16)
    grad_q = (
        jnp.einsum("cgtk,ckd->tcgd", dscores, keys_part, preferred_element_type=jnp.float32)
        * factor
    )
    grad_k = (
        jnp.einsum("cgtk,tcgd->ckd", dscores, q_rows, preferred_element_type=jnp.float32) * factor
    )
    grad_v = jnp.einsum("cgtk,tcgd->ckd", probs_low, grad_rows, preferred_element_type=jnp.float32)
    return (grad_q.astype(jnp.bfloat16), jnp.concatenate([grad_k, grad_v], axis=-1))


def body(query, keys, values, output_cotangent, select):
    seq_count = lax.axis_size("seq")
    group_count = lax.axis_size("grp")
    local_key_value = KEY_HEADS // group_count
    query_group_size = QUERY_HEADS // KEY_HEADS
    rows_q = TOK_DEV * group_count
    qblocks = rows_q // BLOCK_TOKENS
    block_count = select.shape[0]
    stripe = BLOCK_TOKENS // seq_count
    factor = HEAD_SIZE ** (-0.5)
    pair_width = 2 * HEAD_SIZE
    q_heads, g_heads, k_heads, v_heads = (
        lax.all_to_all(query, "grp", split_axis=1, concat_axis=0, tiled=True),
        lax.all_to_all(output_cotangent, "grp", split_axis=1, concat_axis=0, tiled=True),
        lax.all_to_all(keys, "grp", split_axis=1, concat_axis=0, tiled=True),
        lax.all_to_all(values, "grp", split_axis=1, concat_axis=0, tiled=True),
    )
    key_value_pairs = jnp.concatenate(
        [
            k_heads.reshape(rows_q, local_key_value, HEAD_SIZE),
            v_heads.reshape(rows_q, local_key_value, HEAD_SIZE),
        ],
        axis=2,
    )
    spread = lax.all_to_all(
        key_value_pairs.reshape(qblocks, seq_count, stripe, local_key_value, pair_width),
        "seq",
        split_axis=1,
        concat_axis=0,
        tiled=True,
    )
    spread_blocks = spread.reshape(block_count, stripe, local_key_value, pair_width)
    seq_index = lax.axis_index("seq")
    slot_count = CHOSEN_BLOCKS
    head_numbers = jnp.arange(local_key_value, dtype=jnp.int32)[None, None, :, None]
    outgoing = spread_blocks[
        select.reshape(seq_count, qblocks, local_key_value, slot_count), :, head_numbers
    ]
    incoming = lax.all_to_all(outgoing, "seq", split_axis=0, concat_axis=4, tiled=True)
    incoming = incoming.reshape(qblocks, local_key_value, slot_count, BLOCK_TOKENS, pair_width)
    gathered_rows = incoming
    gathered_rows = gathered_rows.reshape(
        qblocks, local_key_value, CHOSEN_BLOCKS * BLOCK_TOKENS, pair_width
    )
    own_select = lax.dynamic_slice_in_dim(select, seq_index * qblocks, qblocks, 0)
    block_offsets = jnp.arange(BLOCK_TOKENS, dtype=jnp.int32)
    key_positions = (own_select[..., None] * BLOCK_TOKENS + block_offsets).reshape(
        qblocks, local_key_value, CHOSEN_BLOCKS * BLOCK_TOKENS
    )
    q_blocks = q_heads.reshape(qblocks, BLOCK_TOKENS, local_key_value, query_group_size, HEAD_SIZE)
    g_blocks = g_heads.reshape(qblocks, BLOCK_TOKENS, local_key_value, query_group_size, HEAD_SIZE)

    def per_block(items):
        q_rows, grad_rows, pairs, positions, block_index = items
        query_pos = (seq_index * qblocks + block_index) * BLOCK_TOKENS + block_offsets
        return block_backward(q_rows, grad_rows, pairs, query_pos, positions, factor)

    grad_q, kv_grads = lax.map(
        per_block,
        (q_blocks, g_blocks, gathered_rows, key_positions, jnp.arange(qblocks, dtype=jnp.int32)),
    )
    grad_query = grad_q.reshape(rows_q, local_key_value * query_group_size * HEAD_SIZE)
    unit_grads = kv_grads.reshape(qblocks, local_key_value, CHOSEN_BLOCKS, BLOCK_TOKENS, pair_width)
    outbound = unit_grads.reshape(
        qblocks, local_key_value, slot_count, seq_count, stripe, pair_width
    )
    returned = lax.all_to_all(outbound, "seq", split_axis=3, concat_axis=0, tiled=True)
    returned = returned.reshape(block_count, local_key_value, slot_count, stripe * pair_width)

    def stripe_sum(data_rows, block_ids):
        return jax.ops.segment_sum(
            data_rows.reshape(block_count * slot_count, stripe * pair_width),
            block_ids.reshape(block_count * slot_count),
            num_segments=block_count,
        )

    total_sums = jax.vmap(stripe_sum, in_axes=(1, 1), out_axes=1)(returned, select)
    total_sums = total_sums.reshape(seq_count, qblocks, local_key_value, stripe, pair_width)
    summed = lax.all_to_all(
        total_sums.astype(jnp.bfloat16), "seq", split_axis=0, concat_axis=3, tiled=True
    )
    summed = summed.reshape(qblocks, local_key_value, BLOCK_TOKENS, pair_width)
    arranged = jnp.transpose(summed, (0, 2, 1, 3))
    key_gradient = arranged[..., :HEAD_SIZE].reshape(rows_q, local_key_value * HEAD_SIZE)
    value_gradient = arranged[..., HEAD_SIZE:].reshape(rows_q, local_key_value * HEAD_SIZE)
    return (grad_query, key_gradient, value_gradient)


def solution(mesh):
    in_specs = (
        P(("seq", "grp"), None),
        P(("seq", "grp"), None),
        P(("seq", "grp"), None),
        P(("seq", "grp"), None),
        P(None, "grp", None),
    )
    out_specs = (P("seq", "grp"), P("seq", "grp"), P("seq", "grp"))
    return jax.shard_map(body, mesh=mesh, in_specs=in_specs, out_specs=out_specs, check_vma=False)
```

profile of v0, /device:TPU:1, one launch (start us, length us, event | category | flops | bytes accessed | tf_op | source)
XLA Modules:
  0.0 795.3 jit_solution(7723270727423738707)
XLA Ops:
  2.6 10.9 %all-to-all-start = ((bf16[128,8,128]{2,0,1:T(8,128)(2,1)}), bf16[128,8,128]{2,0,1:T(8,128)(2,1)S(1)}, u32[]{:S(2)}, u32[]{:S(2)}) async-start(bf16[128,8,128]{2,0,1:T(8,128)(2,1)} %copy.168), calls=%async_computation | async-start | bytes 524288 | tf_op jit(solution)/shard_map/all_to_all | solution.py:59
  15.5 8.4 %all-to-all-done = bf16[128,8,128]{2,0,1:T(8,128)(2,1)S(1)} async-done(((bf16[128,8,128]{2,0,1:T(8,128)(2,1)}), bf16[128,8,128]{2,0,1:T(8,128)(2,1)S(1)}, u32[]{:S(2)}, u32[]{:S(2)}) %all-to-all-start) | async-done | bytes 262176 | tf_op jit(solution)/shard_map/all_to_all | solution.py:59
  27.4 9.2 %all-to-all-done.1 = bf16[128,8,128]{2,0,1:T(8,128)(2,1)S(1)} async-done(((bf16[128,8,128]{2,0,1:T(8,128)(2,1)}), bf16[128,8,128]{2,0,1:T(8,128)(2,1)S(1)}, u32[]{:S(2)}, u32[]{:S(2)}) %all-to-all-start.1) | async-done | bytes 262176 | tf_op jit(solution)/shard_map/all_to_all | solution.py:60
  37.7 13.6 %all-to-all-start.2 = ((bf16[8,64,2,1,256]{4,0,2,3,1:T(8,128)(2,1)}), bf16[8,64,2,1,256]{4,0,2,3,1:T(8,128)(2,1)S(1)}, u32[]{:S(2)}, u32[]{:S(2)}) async-start(bf16[8,64,2,1,256]{4,0,2,3,1:T(8,128)(2,1)} %maximum_bitcast_fusion.1), calls=%async_computation.2 | async-start | bytes 1048576 | tf_op jit(solution)/shard_map/all_to_all | solution.py:69
  52.7 16.4 %all-to-all-done.2 = bf16[8,64,2,1,256]{4,0,2,3,1:T(8,128)(2,1)S(1)} async-done(((bf16[8,64,2,1,256]{4,0,2,3,1:T(8,128)(2,1)}), bf16[8,64,2,1,256]{4,0,2,3,1:T(8,128)(2,1)S(1)}, u32[]{:S(2)}, u32[]{:S(2)}) %all-to-all-start.2) | async-done | bytes 524320 | tf_op jit(solution)/shard_map/all_to_all | solution.py:69
  73.9 33.2 %gather_fusion = bf16[4096,2,256]{2,1,0:T(2,128)(2,1)} fusion(bf16[512,2,1,256]{3,1,2,0:T(2,128)(2,1)S(1)} %copy.179, s32[4096]{0:T(1024)S(1)} %reshape.325), kind=kCustom, calls=%fused_computation | custom fusion | bytes 8421376 | tf_op jit(solution)/shard_map/gather | solution.py:80
  119.5 93.1 %all-to-all-done.3 = bf16[64,8,1,8,2,256]{5,3,1,4,2,0:T(8,128)(2,1)} async-done(((bf16[64,8,1,8,2,256]{5,3,1,4,2,0:T(8,128)(2,1)}), bf16[64,8,1,8,2,256]{5,3,1,4,2,0:T(8,128)(2,1)}, u32[]{:S(2)}, u32[]{:S(2)}) %all-to-all-start.3) | async-done | bytes 4194336 | tf_op jit(solution)/shard_map/all_to_all | solution.py:83
  225.6 21.2 %all-to-all-done.5 = bf16[128,8,512]{0,2,1:T(8,128)(2,1)} async-done(((bf16[128,8,512]{0,2,1:T(8,128)(2,1)}), bf16[128,8,512]{0,2,1:T(8,128)(2,1)}, u32[]{:S(2)}, u32[]{:S(2)}) %all-to-all-start.5) | async-done | bytes 1048608 | tf_op jit(solution)/shard_map/all_to_all | solution.py:58
  246.9 276.3 %while.15 = (s32[]{:T(128)}, bf16[8,128,1,4,128]{4,3,1,0,2:T(4,128)(2,1)}, f32[8,1,1024,256]{3,0,2,1:T(8,128)}, bf16[8,1,1024,256]{3,2,1,0:T(8,128)(2,1)}, s32[8...) while((s32[]{:T(128)}, ...), condition=%wide.region_4.5_spmd.clone, body=%wide.region_0.4_spmd.clone.sunk | while | flops 812972672 | bytes 25984256 | solution.py:102
  257.4 24.0 %dynamic_update_slice.18 = f32[8,1,1024,256]{3,0,2,1:T(8,128)} dynamic-update-slice(f32[8,1,1024,256]{3,0,2,1:T(8,128)} %get-tuple-element.291, f32[1,1,1024,256]{3,0,2,1:T(1,128)S(1)} %copy.226, s32[]{:T(128)S(6)} %copy.232, s32[]{:T(128)} %constant.58.clone.1..sunk, s32[]{:T(128)} %constant.58.clone.1..sunk, s32[]{:T(128)} %constant.58.clone.1..sunk) | dynamic-update-slice | bytes 2097156 | tf_op jit(solution)/shard_map/while/body/jit(dynamic_update_index_in_dim)/dynamic_update_slice | solution.py:102
  291.9 24.0 %dynamic_update_slice.18 = f32[8,1,1024,256]{3,0,2,1:T(8,128)} dynamic-update-slice(f32[8,1,1024,256]{3,0,2,1:T(8,128)} %get-tuple-element.291, f32[1,1,1024,256]{3,0,2,1:T(1,128)S(1)} %copy.226, s32[]{:T(128)S(6)} %copy.232, s32[]{:T(128)} %constant.58.clone.1..sunk, s32[]{:T(128)} %constant.58.clone.1..sunk, s32[]{:T(128)} %constant.58.clone.1..sunk) | dynamic-update-slice | bytes 2097156 | tf_op jit(solution)/shard_map/while/body/jit(dynamic_update_index_in_dim)/dynamic_update_slice | solution.py:102
  326.5 24.0 %dynamic_update_slice.18 = f32[8,1,1024,256]{3,0,2,1:T(8,128)} dynamic-update-slice(f32[8,1,1024,256]{3,0,2,1:T(8,128)} %get-tuple-element.291, f32[1,1,1024,256]{3,0,2,1:T(1,128)S(1)} %copy.226, s32[]{:T(128)S(6)} %copy.232, s32[]{:T(128)} %constant.58.clone.1..sunk, s32[]{:T(128)} %constant.58.clone.1..sunk, s32[]{:T(128)} %constant.58.clone.1..sunk) | dynamic-update-slice | bytes 2097156 | tf_op jit(solution)/shard_map/while/body/jit(dynamic_update_index_in_dim)/dynamic_update_slice | solution.py:102
  361.0 24.0 %dynamic_update_slice.18 = f32[8,1,1024,256]{3,0,2,1:T(8,128)} dynamic-update-slice(f32[8,1,1024,256]{3,0,2,1:T(8,128)} %get-tuple-element.291, f32[1,1,1024,256]{3,0,2,1:T(1,128)S(1)} %copy.226, s32[]{:T(128)S(6)} %copy.232, s32[]{:T(128)} %constant.58.clone.1..sunk, s32[]{:T(128)} %constant.58.clone.1..sunk, s32[]{:T(128)} %constant.58.clone.1..sunk) | dynamic-update-slice | bytes 2097156 | tf_op jit(solution)/shard_map/while/body/jit(dynamic_update_index_in_dim)/dynamic_update_slice | solution.py:102
  395.6 24.0 %dynamic_update_slice.18 = f32[8,1,1024,256]{3,0,2,1:T(8,128)} dynamic-update-slice(f32[8,1,1024,256]{3,0,2,1:T(8,128)} %get-tuple-element.291, f32[1,1,1024,256]{3,0,2,1:T(1,128)S(1)} %copy.226, s32[]{:T(128)S(6)} %copy.232, s32[]{:T(128)} %constant.58.clone.1..sunk, s32[]{:T(128)} %constant.58.clone.1..sunk, s32[]{:T(128)} %constant.58.clone.1..sunk) | dynamic-update-slice | bytes 2097156 | tf_op jit(solution)/shard_map/while/body/jit(dynamic_update_index_in_dim)/dynamic_update_slice | solution.py:102
  430.1 24.0 %dynamic_update_slice.18 = f32[8,1,1024,256]{3,0,2,1:T(8,128)} dynamic-update-slice(f32[8,1,1024,256]{3,0,2,1:T(8,128)} %get-tuple-element.291, f32[1,1,1024,256]{3,0,2,1:T(1,128)S(1)} %copy.226, s32[]{:T(128)S(6)} %copy.232, s32[]{:T(128)} %constant.58.clone.1..sunk, s32[]{:T(128)} %constant.58.clone.1..sunk, s32[]{:T(128)} %constant.58.clone.1..sunk) | dynamic-update-slice | bytes 2097156 | tf_op jit(solution)/shard_map/while/body/jit(dynamic_update_index_in_dim)/dynamic_update_slice | solution.py:102
  464.6 24.0 %dynamic_update_slice.18 = f32[8,1,1024,256]{3,0,2,1:T(8,128)} dynamic-update-slice(f32[8,1,1024,256]{3,0,2,1:T(8,128)} %get-tuple-element.291, f32[1,1,1024,256]{3,0,2,1:T(1,128)S(1)} %copy.226, s32[]{:T(128)S(6)} %copy.232, s32[]{:T(128)} %constant.58.clone.1..sunk, s32[]{:T(128)} %constant.58.clone.1..sunk, s32[]{:T(128)} %constant.58.clone.1..sunk) | dynamic-update-slice | bytes 2097156 | tf_op jit(solution)/shard_map/while/body/jit(dynamic_update_index_in_dim)/dynamic_update_slice | solution.py:102
  499.2 24.0 %dynamic_update_slice.18 = f32[8,1,1024,256]{3,0,2,1:T(8,128)} dynamic-update-slice(f32[8,1,1024,256]{3,0,2,1:T(8,128)} %get-tuple-element.291, f32[1,1,1024,256]{3,0,2,1:T(1,128)S(1)} %copy.226, s32[]{:T(128)S(6)} %copy.232, s32[]{:T(128)} %constant.58.clone.1..sunk, s32[]{:T(128)} %constant.58.clone.1..sunk, s32[]{:T(128)} %constant.58.clone.1..sunk) | dynamic-update-slice | bytes 2097156 | tf_op jit(solution)/shard_map/while/body/jit(dynamic_update_index_in_dim)/dynamic_update_slice | solution.py:102
  523.2 8.1 %copy.191 = f32[8,1,8,64,2,256]{5,0,4,2,1,3:T(8,128)} copy(f32[8,1,8,64,2,256]{5,0,4,3,2,1:T(8,128)} %bitcast.215) | data formatting | bytes 16777216 | tf_op jit(solution)/shard_map/reshape;reshape | solution.py:108
  531.3 9.4 %all-to-all-start.6 = ((f32[8,1,8,64,2,256]{5,0,4,2,1,3:T(8,128)}), f32[8,1,8,64,2,256]{5,0,4,2,1,3:T(8,128)}, u32[]{:S(2)}, u32[]{:S(2)}) async-start(f32[8,1,8,64,2,256]{5,0,4,2,1,3:T(8,128)} %copy.191), calls=%async_computation.6 | async-start | bytes 16777216 | tf_op jit(solution)/shard_map/all_to_all | solution.py:111
  541.1 182.0 %all-to-all-done.6 = f32[8,1,8,64,2,256]{5,0,4,2,1,3:T(8,128)} async-done(((f32[8,1,8,64,2,256]{5,0,4,2,1,3:T(8,128)}), f32[8,1,8,64,2,256]{5,0,4,2,1,3:T(8,128)}, u32[]{:S(2)}, u32[]{:S(2)}) %all-to-all-start.6) | async-done | bytes 8388640 | tf_op jit(solution)/shard_map/all_to_all | solution.py:111
  723.1 12.2 %copy.192 = f32[64,8,1,8,1,2,256]{6,5,3,1,0,4,2:T(2,128)S(1)} copy(f32[64,8,1,8,1,2,256]{6,1,5,3,0,4,2:T(8,128)} %bitcast.26) | data formatting | bytes 16777216 | tf_op jit(solution)/shard_map/all_to_all | solution.py:111
  739.5 25.4 %scatter_custom_fusion = f32[512,512]{1,0:T(8,128)S(1)} fusion(s32[4096]{0:T(1024)S(1)} %broadcast_select_fusion, f32[4096,512]{1,0:T(8,128)} %bitcast.216, f32[]{:T(128)} %constant.60.clone.1), kind=kCustom, calls=%fused_computation.47 | custom fusion | flops 2097152 | bytes 1049088
  765.9 10.0 %all-to-all-start.7 = ((bf16[64,8,1,2,256]{4,3,1,2,0:T(2,128)(2,1)}), bf16[64,8,1,2,256]{4,3,1,2,0:T(2,128)(2,1)S(1)}, u32[]{:S(2)}, u32[]{:S(2)}) async-start(bf16[64,8,1,2,256]{4,3,1,2,0:T(2,128)(2,1)} %bitcast.27), calls=%async_computation.7 | async-start | bytes 1048576 | tf_op jit(solution)/shard_map/all_to_all | solution.py:123
  777.1 16.6 %all-to-all-done.7 = bf16[64,8,1,2,256]{4,3,1,2,0:T(2,128)(2,1)S(1)} async-done(((bf16[64,8,1,2,256]{4,3,1,2,0:T(2,128)(2,1)}), bf16[64,8,1,2,256]{4,3,1,2,0:T(2,128)(2,1)S(1)}, u32[]{:S(2)}, u32[]{:S(2)}) %all-to-all-start.7) | async-done | bytes 524320 | tf_op jit(solution)/shard_map/all_to_all | solution.py:123
  (226 shorter events, 126.2 us)
Async XLA Ops:
  2.6 21.2 %all-to-all-start = ((bf16[128,8,128]{2,0,1:T(8,128)(2,1)}), bf16[128,8,128]{2,0,1:T(8,128)(2,1)S(1)}, u32[]{:S(2)}, u32[]{:S(2)}) async-start(bf16[128,8,128]{2,0,1:T(8,128)(2,1)} %copy.168), calls=%async_computation | async-start | bytes 524288 | tf_op jit(solution)/shard_map/all_to_all | solution.py:59
  14.6 36.7 %copy-start = (bf16[128,4096]{1,0:T(8,128)(2,1)S(1)}, bf16[128,4096]{1,0:T(8,128)(2,1)}, u32[]{:S(2)}) copy-start(bf16[128,4096]{1,0:T(8,128)(2,1)} %param.7) | copy-start | bytes 3145732
  23.8 12.8 %all-to-all-start.1 = ((bf16[128,8,128]{2,0,1:T(8,128)(2,1)}), bf16[128,8,128]{2,0,1:T(8,128)(2,1)S(1)}, u32[]{:S(2)}, u32[]{:S(2)}) async-start(bf16[128,8,128]{2,0,1:T(8,128)(2,1)} %copy.171), calls=%async_computation.1 | async-start | bytes 524288 | tf_op jit(solution)/shard_map/all_to_all | solution.py:60
  37.7 31.3 %all-to-all-start.2 = ((bf16[8,64,2,1,256]{4,0,2,3,1:T(8,128)(2,1)}), bf16[8,64,2,1,256]{4,0,2,3,1:T(8,128)(2,1)S(1)}, u32[]{:S(2)}, u32[]{:S(2)}) async-start(bf16[8,64,2,1,256]{4,0,2,3,1:T(8,128)(2,1)} %maximum_bitcast_fusion.1), calls=%async_computation.2 | async-start | bytes 1048576 | tf_op jit(solution)/shard_map/all_to_all | solution.py:69
  51.3 21.3 %copy-start.5 = (s32[512,1,8]{0,2,1:T(8,128)S(1)}, s32[512,1,8]{0,2,1:T(8,128)}, u32[]{:S(2)}) copy-start(s32[512,1,8]{0,2,1:T(8,128)} %param.11) | copy-start | bytes 49156
  69.1 43.1 %all-to-all-start.4 = ((bf16[128,8,512]{0,2,1:T(8,128)(2,1)}), bf16[128,8,512]{0,2,1:T(8,128)(2,1)S(1)}, u32[]{:S(2)}, u32[]{:S(2)}) async-start(bf16[128,8,512]{0,2,1:T(8,128)(2,1)} %bitcast.18), calls=%async_computation.4 | async-start | bytes 2097152 | tf_op jit(solution)/shard_map/all_to_all | solution.py:57
  112.2 6.1 copy-start.1
  112.2 100.5 %all-to-all-start.3 = ((bf16[64,8,1,8,2,256]{5,3,1,4,2,0:T(8,128)(2,1)}), bf16[64,8,1,8,2,256]{5,3,1,4,2,0:T(8,128)(2,1)}, u32[]{:S(2)}, u32[]{:S(2)}) async-start(bf16[64,8,1,8,2,256]{5,3,1,4,2,0:T(8,128)(2,1)} %copy.181), calls=%async_computation.3 | async-start | bytes 8388608 | tf_op jit(solution)/shard_map/all_to_all | solution.py:83
  212.6 34.2 %all-to-all-start.5 = ((bf16[128,8,512]{0,2,1:T(8,128)(2,1)}), bf16[128,8,512]{0,2,1:T(8,128)(2,1)}, u32[]{:S(2)}, u32[]{:S(2)}) async-start(bf16[128,8,512]{0,2,1:T(8,128)(2,1)} %bitcast.21), calls=%async_computation.5 | async-start | bytes 2097152 | tf_op jit(solution)/shard_map/all_to_all | solution.py:58
  246.9 3.4 copy-start.3
  256.7 24.7 %copy-start.4 = (s32[8,1,1024]{2,1,0:T(1,128)S(1)}, s32[8,1,1024]{2,1,0:T(1,128)}, u32[]{:S(2)}) copy-start(s32[8,1,1024]{2,1,0:T(1,128)} %copy-done.3) | copy-start | bytes 98308 | tf_op jit(solution)/shard_map/while
  291.2 24.7 %copy-start.4 = (s32[8,1,1024]{2,1,0:T(1,128)S(1)}, s32[8,1,1024]{2,1,0:T(1,128)}, u32[]{:S(2)}) copy-start(s32[8,1,1024]{2,1,0:T(1,128)} %copy-done.3) | copy-start | bytes 98308 | tf_op jit(solution)/shard_map/while
  315.9 3.4 copy-start.3
  325.8 24.7 %copy-start.4 = (s32[8,1,1024]{2,1,0:T(1,128)S(1)}, s32[8,1,1024]{2,1,0:T(1,128)}, u32[]{:S(2)}) copy-start(s32[8,1,1024]{2,1,0:T(1,128)} %copy-done.3) | copy-start | bytes 98308 | tf_op jit(solution)/shard_map/while
  360.3 24.7 %copy-start.4 = (s32[8,1,1024]{2,1,0:T(1,128)S(1)}, s32[8,1,1024]{2,1,0:T(1,128)}, u32[]{:S(2)}) copy-start(s32[8,1,1024]{2,1,0:T(1,128)} %copy-done.3) | copy-start | bytes 98308 | tf_op jit(solution)/shard_map/while
  394.8 24.7 %copy-start.4 = (s32[8,1,1024]{2,1,0:T(1,128)S(1)}, s32[8,1,1024]{2,1,0:T(1,128)}, u32[]{:S(2)}) copy-start(s32[8,1,1024]{2,1,0:T(1,128)} %copy-done.3) | copy-start | bytes 98308 | tf_op jit(solution)/shard_map/while
  429.4 24.7 %copy-start.4 = (s32[8,1,1024]{2,1,0:T(1,128)S(1)}, s32[8,1,1024]{2,1,0:T(1,128)}, u32[]{:S(2)}) copy-start(s32[8,1,1024]{2,1,0:T(1,128)} %copy-done.3) | copy-start | bytes 98308 | tf_op jit(solution)/shard_map/while
  463.9 24.7 %copy-start.4 = (s32[8,1,1024]{2,1,0:T(1,128)S(1)}, s32[8,1,1024]{2,1,0:T(1,128)}, u32[]{:S(2)}) copy-start(s32[8,1,1024]{2,1,0:T(1,128)} %copy-done.3) | copy-start | bytes 98308 | tf_op jit(solution)/shard_map/while
  498.5 24.7 %copy-start.4 = (s32[8,1,1024]{2,1,0:T(1,128)S(1)}, s32[8,1,1024]{2,1,0:T(1,128)}, u32[]{:S(2)}) copy-start(s32[8,1,1024]{2,1,0:T(1,128)} %copy-done.3) | copy-start | bytes 98308 | tf_op jit(solution)/shard_map/while
  531.3 9.6 %copy-start.6 = (s32[2]{0:T(128)S(1)}, s32[2]{0:T(128)}, u32[]{:S(2)}) copy-start(s32[2]{0:T(128)} %constant.73) | copy-start | bytes 28
  531.3 9.7 %copy-start.7 = (s32[2]{0:T(128)S(1)}, s32[2]{0:T(128)}, u32[]{:S(2)}) copy-start(s32[2]{0:T(128)} %constant.76) | copy-start | bytes 28
  531.3 191.8 %all-to-all-start.6 = ((f32[8,1,8,64,2,256]{5,0,4,2,1,3:T(8,128)}), f32[8,1,8,64,2,256]{5,0,4,2,1,3:T(8,128)}, u32[]{:S(2)}, u32[]{:S(2)}) async-start(f32[8,1,8,64,2,256]{5,0,4,2,1,3:T(8,128)} %copy.191), calls=%async_computation.6 | async-start | bytes 16777216 | tf_op jit(solution)/shard_map/all_to_all | solution.py:111
  764.9 11.0 %copy-start.2 = (bf16[8,128,1,4,128]{4,3,1,0,2:T(4,128)(2,1)S(1)}, bf16[8,128,1,4,128]{4,3,1,0,2:T(4,128)(2,1)}, u32[]{:S(2)}) copy-start(bf16[8,128,1,4,128]{4,3,1,0,2:T(4,128)(2,1)} %get-tuple-element.120) | copy-start | bytes 3145732
  765.9 27.7 %all-to-all-start.7 = ((bf16[64,8,1,2,256]{4,3,1,2,0:T(2,128)(2,1)}), bf16[64,8,1,2,256]{4,3,1,2,0:T(2,128)(2,1)S(1)}, u32[]{:S(2)}, u32[]{:S(2)}) async-start(bf16[64,8,1,2,256]{4,3,1,2,0:T(2,128)(2,1)} %bitcast.27), calls=%async_computation.7 | async-start | bytes 1048576 | tf_op jit(solution)/shard_map/all_to_all | solution.py:123
  (6 other events, 20.6 us)
where the time goes:
time: 802 us; the launch traced here: 795 us
  waiting for transfers between devices  347 us (43%)
  local copies, waits for them, and re-layouts  300 us (37%)
  starting transfers between devices  63.7 us (8%)
  matrix products  43.1 us (5%)
  other arithmetic  34.4 us (4%)
    dynamic_update_slice x32, local copies, waits for them, and re-layouts, body(): lax.map(per_block, (q_blocks, g_blocks, gathered_rows, key_positions, jnp...  205 us
    all_to_all x1, waiting for transfers between devices, body(): lax.all_to_all(outbound, 'seq', split_axis=3, concat_axis=0, tiled=True)  182 us
    all_to_all x1, waiting for transfers between devices, body(): lax.all_to_all(outgoing, 'seq', split_axis=0, concat_axis=4, tiled=True)  93.1 us
    gather x2, local copies, waits for them, and re-layouts, body(): spread_blocks[select.reshape(seq_count, qblocks, local_key_value, slot_co...  38.3 us
    unnamed x4, other arithmetic  25.7 us
    all_to_all x1, waiting for transfers between devices, body(): lax.all_to_all(output_cotangent, 'grp', split_axis=1, concat_axis=0, tile...  21.2 us
    all_to_all x1, waiting for transfers between devices, body(): lax.all_to_all(total_sums.astype(jnp.bfloat16), 'seq', split_axis=0, conc...  16.6 us
    all_to_all x1, waiting for transfers between devices, body(): lax.all_to_all(key_value_pairs.reshape(qblocks, seq_count, stripe, local_...  16.4 us
  transfers between devices with their start and end apart: 8, of which 7 were waited for; matrix products, arithmetic and copies ran while one was open for 7% of the time, Pallas kernels for 0%

commit v1 on v0

v1 whole, which is shorter than its diff:
```python
import functools

import jax
import jax.numpy as jnp
from jax import lax
from jax.experimental import pallas as pl
from jax.experimental.pallas import tpu as pltpu
from jax.sharding import PartitionSpec as P

HEAD_SIZE = 128
QUERY_HEADS = 32
KEY_HEADS = 8
BLOCK_TOKENS = 128
CHOSEN_BLOCKS = 8
GROUP = QUERY_HEADS // KEY_HEADS
PAIR = 2 * HEAD_SIZE
STRIPES = 8
ROWS = BLOCK_TOKENS // STRIPES
KEYS = CHOSEN_BLOCKS * BLOCK_TOKENS
FACTOR = HEAD_SIZE ** (-0.5)
VMEM = 56 * 1024 * 1024


def pack_kernel(sel, table, out):
    @pl.loop(0, sel.shape[0], unroll=8)
    def _(r):
        out[r] = table[sel[r]]


def accumulate_kernel(sel, rows, out, total):
    total[...] = jnp.zeros_like(total)

    @pl.loop(0, sel.shape[0], unroll=8)
    def _(r):
        total[sel[r]] += rows[r].astype(jnp.float32)

    out[...] = total[...].astype(out.dtype)


def nt(a, b):
    return lax.dot_general(a, b, (((1,), (1,)), ((), ())), preferred_element_type=jnp.float32)


def nn(a, b):
    return jnp.dot(a, b, preferred_element_type=jnp.float32)


def attention_kernel(sel, q_ref, g_ref, kv_ref, dq_ref, dkv_ref, probs, dscores):
    step = pl.program_id(0)
    keys = kv_ref[:, 0, :, :, :HEAD_SIZE].reshape(KEYS, HEAD_SIZE)
    vals = kv_ref[:, 0, :, :, HEAD_SIZE:].reshape(KEYS, HEAD_SIZE)
    stripe = lax.broadcasted_iota(jnp.int32, (STRIPES, ROWS, BLOCK_TOKENS), 0)
    row = lax.broadcasted_iota(jnp.int32, (STRIPES, ROWS, BLOCK_TOKENS), 1)
    token = lax.broadcasted_iota(jnp.int32, (STRIPES, ROWS, BLOCK_TOKENS), 2)
    ahead = stripe * ROWS + row - token
    own = sel[step * CHOSEN_BLOCKS]
    bias = jnp.stack(
        [
            jnp.where(
                ahead <= (own - sel[step * CHOSEN_BLOCKS + j]) * BLOCK_TOKENS, 0.0, -jnp.inf
            ).astype(jnp.float32)
            for j in range(CHOSEN_BLOCKS)
        ],
        axis=1,
    ).reshape(KEYS, BLOCK_TOKENS)
    for h in range(GROUP):
        cols = pl.ds(h * HEAD_SIZE, HEAD_SIZE)
        q, g = q_ref[:, cols], g_ref[:, cols]
        scores = nt(keys, q) * FACTOR + bias
        highest = jnp.max(scores, axis=0, keepdims=True)
        weights = jnp.exp(scores - highest)
        prob = weights * (1.0 / jnp.sum(weights, axis=0, keepdims=True))
        low = prob.astype(jnp.bfloat16)
        dprobs = nt(vals, g)
        delta = jnp.sum(low.astype(jnp.float32) * dprobs, axis=0, keepdims=True)
        probs[:, cols] = low
        dscores[:, cols] = (prob * (dprobs - delta)).astype(jnp.bfloat16)
    q_rows = jnp.concatenate([q_ref[:, h * HEAD_SIZE : (h + 1) * HEAD_SIZE] for h in range(GROUP)], 0)
    g_rows = jnp.concatenate([g_ref[:, h * HEAD_SIZE : (h + 1) * HEAD_SIZE] for h in range(GROUP)], 0)
    dk = nn(dscores[...], q_rows) * FACTOR
    dv = nn(probs[...], g_rows)
    full = (STRIPES, CHOSEN_BLOCKS, ROWS, HEAD_SIZE)
    dkv_ref[:, 0, :, :, :HEAD_SIZE] = dk.astype(jnp.bfloat16).reshape(full)
    dkv_ref[:, 0, :, :, HEAD_SIZE:] = dv.astype(jnp.bfloat16).reshape(full)
    dq_t = nn(keys.T, dscores[...]) * FACTOR
    for h in range(GROUP):
        cols = pl.ds(h * HEAD_SIZE, HEAD_SIZE)
        dq_ref[:, cols] = dq_t[:, h * HEAD_SIZE : (h + 1) * HEAD_SIZE].T.astype(jnp.bfloat16)


def pack(sel, table):
    return pl.pallas_call(
        pack_kernel,
        out_shape=jax.ShapeDtypeStruct((sel.shape[0],) + table.shape[1:], table.dtype),
        in_specs=[
            pl.BlockSpec(memory_space=pltpu.SMEM),
            pl.BlockSpec(memory_space=pltpu.VMEM),
        ],
        out_specs=pl.BlockSpec(memory_space=pltpu.VMEM),
        compiler_params=pltpu.CompilerParams(vmem_limit_bytes=VMEM),
        name="pack",
    )(sel, table)


def accumulate(sel, rows, blocks):
    return pl.pallas_call(
        accumulate_kernel,
        out_shape=jax.ShapeDtypeStruct((blocks,) + rows.shape[1:], rows.dtype),
        in_specs=[
            pl.BlockSpec(memory_space=pltpu.SMEM),
            pl.BlockSpec(memory_space=pltpu.VMEM),
        ],
        out_specs=pl.BlockSpec(memory_space=pltpu.VMEM),
        scratch_shapes=[pltpu.VMEM((blocks,) + rows.shape[1:], jnp.float32)],
        compiler_params=pltpu.CompilerParams(vmem_limit_bytes=VMEM),
        name="accumulate",
    )(sel, rows)


def attention(sel, q, g, kv):
    steps = kv.shape[1]
    rows = pl.BlockSpec((BLOCK_TOKENS, GROUP * HEAD_SIZE), lambda i, s: (i, 0))
    pairs = pl.BlockSpec((STRIPES, 1, CHOSEN_BLOCKS, ROWS, PAIR), lambda i, s: (0, i, 0, 0, 0))
    return pl.pallas_call(
        attention_kernel,
        out_shape=(
            jax.ShapeDtypeStruct(q.shape, jnp.bfloat16),
            jax.ShapeDtypeStruct(kv.shape, jnp.bfloat16),
        ),
        grid_spec=pltpu.PrefetchScalarGridSpec(
            num_scalar_prefetch=1,
            grid=(steps,),
            in_specs=[rows, rows, pairs],
            out_specs=[rows, pairs],
            scratch_shapes=[pltpu.VMEM((KEYS, GROUP * BLOCK_TOKENS), jnp.bfloat16)] * 2,
        ),
        compiler_params=pltpu.CompilerParams(vmem_limit_bytes=VMEM),
        name="attention",
    )(sel, q, g, kv)


def body(query, keys, values, output_cotangent, select):
    qblocks = lax.axis_size("grp")
    columns = lax.axis_size("xc")
    row_blocks = columns * qblocks
    blocks = select.shape[0]
    row = lax.axis_index("y")
    column = lax.axis_index("xc")
    flat = select.reshape(blocks * CHOSEN_BLOCKS)
    width = row_blocks * CHOSEN_BLOCKS
    row_select = lax.dynamic_slice_in_dim(flat, row * width, width, 0)
    own_select = lax.dynamic_slice_in_dim(
        flat, row * width + column * qblocks * CHOSEN_BLOCKS, qblocks * CHOSEN_BLOCKS, 0
    )
    pairs = jnp.concatenate(
        [
            keys.reshape(columns, ROWS, KEY_HEADS, HEAD_SIZE),
            values.reshape(columns, ROWS, KEY_HEADS, HEAD_SIZE),
        ],
        axis=3,
    )
    pairs = jnp.transpose(pairs, (0, 2, 1, 3)).reshape(columns * KEY_HEADS, ROWS, PAIR)
    share = lax.all_to_all(pairs, ("xc", "grp"), split_axis=0, concat_axis=0, tiled=True)
    table = lax.all_gather(share, "y", axis=0, tiled=True)
    q_heads = lax.all_to_all(query, "grp", split_axis=1, concat_axis=0, tiled=True)
    g_heads = lax.all_to_all(output_cotangent, "grp", split_axis=1, concat_axis=0, tiled=True)
    outgoing = pack(row_select, table)
    incoming = lax.all_to_all(outgoing, "xc", split_axis=0, concat_axis=0, tiled=True)
    incoming = incoming.reshape(columns, qblocks, CHOSEN_BLOCKS, ROWS, PAIR)
    grad_query, unit_grads = attention(own_select, q_heads, g_heads, incoming)
    returned = lax.all_to_all(
        unit_grads.reshape(width, ROWS, PAIR), "xc", split_axis=0, concat_axis=0, tiled=True
    )
    sums = accumulate(row_select, returned, blocks)
    row_sums = lax.psum_scatter(sums, "y", scatter_dimension=0, tiled=True)
    own = lax.all_to_all(row_sums, "xc", split_axis=0, concat_axis=0, tiled=True)
    own = jnp.transpose(own.reshape(columns, qblocks, ROWS, PAIR), (1, 0, 2, 3))
    own = own.reshape(qblocks * BLOCK_TOKENS, PAIR)
    return grad_query, own[:, :HEAD_SIZE], own[:, HEAD_SIZE:]


def solution(mesh):
    groups = mesh.shape["grp"]
    grid = jax.sharding.Mesh(
        mesh.devices.reshape(-1, STRIPES, groups), ("y", "xc", "grp")
    )
    rows = ("y", "xc")
    in_specs = (P(rows + ("grp",), None),) * 4 + (P(None, "grp", None),)
    out_specs = (P(rows, "grp"),) * 3
    return jax.shard_map(
        body, mesh=grid, in_specs=in_specs, out_specs=out_specs, check_vma=False
    )
```

time: 802 us -> 322 us (0.40)
  local copies, waits for them, and re-layouts: 300 us -> 6.78 us
  waiting for transfers between devices: 347 us -> 152 us
  blocking collectives: 0 us -> 101 us
  starting transfers between devices: 63.7 us -> 12.8 us
  matrix products: 43.1 us -> 0 us
  Pallas kernels: 0 us -> 35 us
  other arithmetic: 34.4 us -> 0.07 us
  between operations: 0.95 us -> 14.2 us
    all_to_all x6 -> x1, waiting for transfers between devices: 326 us -> 48.3 us  [body(): lax.all_to_all(outgoing, 'xc', split_axis=0, concat_axis=0, tiled=True)]
    dynamic_update_slice x32 -> x0, local copies, waits for them, and re-layouts: 205 us -> none  [body(): lax.map(per_block, (q_blocks, g_blocks, gathered_rows, key_positions, jnp...]
    all_to_all x0 -> x3, blocking collectives: none -> 101 us  [the longest x1 54.6 us: body(): lax.all_to_all(unit_grads.reshape(width, ROWS, PAIR), 'xc', split_axis=0,...]
    reduce_scatter x0 -> x1, waiting for transfers between devices: none -> 52.5 us  [body(): row_sums = lax.psum_scatter(sums, 'y', scatter_dimension=0, tiled=True)]
    all_to_all x6 -> x1, starting transfers between devices: 53.3 us -> 4.91 us  [body(): lax.all_to_all(outgoing, 'xc', split_axis=0, concat_axis=0, tiled=True)]
    dot_general x48 -> x0, matrix products: 43.1 us -> none  [the longest x8 11.9 us: block_backward(): jnp.einsum('tcgd,ckd->cgtk', grad_rows, vals_part, preferred_element_type...]
    gather x2 -> x0, local copies, waits for them, and re-layouts: 38.3 us -> none  [body(): spread_blocks[select.reshape(seq_count, qblocks, local_key_value, slot_co...]
    pallas_call x0 -> x3, Pallas kernels: none -> 35 us  [the longest x1 23 us: attention(): pl.pallas_call(attention_kernel, out_shape=(jax.ShapeDtypeStruct(q.shape,...]
  transfers between devices with their start and end apart: 8 -> 5, of which waited for: 7 -> 5; matrix products, arithmetic and copies ran while one was open for 7% -> 1% of each run, Pallas kernels for 0% -> 2%
where the time goes in v1:
time: 322 us
  waiting for transfers between devices  152 us (47%)
  blocking collectives  101 us (31%)
  Pallas kernels  35 us (11%)
  between operations  14.2 us (4%)
  starting transfers between devices  12.8 us (4%)
  local copies, waits for them, and re-layouts  6.78 us (2%)
    all_to_all x1, blocking collectives, body(): lax.all_to_all(unit_grads.reshape(width, ROWS, PAIR), 'xc', split_axis=0,...  54.6 us
    reduce_scatter x1, waiting for transfers between devices, body(): row_sums = lax.psum_scatter(sums, 'y', scatter_dimension=0, tiled=True)  52.5 us
    all_to_all x1, waiting for transfers between devices, body(): lax.all_to_all(outgoing, 'xc', split_axis=0, concat_axis=0, tiled=True)  48.3 us
    all_to_all x1, blocking collectives, body(): lax.all_to_all(pairs, ('xc', 'grp'), split_axis=0, concat_axis=0, tiled=T...  31.8 us
    all_to_all x1, waiting for transfers between devices, body(): lax.all_to_all(query, 'grp', split_axis=1, concat_axis=0, tiled=True)  28.2 us
    pallas_call x1, Pallas kernels, attention(): pl.pallas_call(attention_kernel, out_shape=(jax.ShapeDtypeStruct(q.shape,...  23 us
    all_gather x1, waiting for transfers between devices, body(): table = lax.all_gather(share, 'y', axis=0, tiled=True)  15.3 us
    all_to_all x1, blocking collectives, body(): lax.all_to_all(row_sums, 'xc', split_axis=0, concat_axis=0, tiled=True)  14.2 us
  transfers between devices with their start and end apart: 5, of which 5 were waited for; matrix products, arithmetic and copies ran while one was open for 1% of the time, Pallas kernels for 2%

profile of v1, /device:TPU:1, one launch (start us, length us, event | category | flops | bytes accessed | tf_op | source)
XLA Modules:
  0.0 321.7 jit_solution(11013664064535871852)
XLA Ops:
  7.2 1.1 copy.27
  8.4 1.1 copy.28
  9.5 0.1 pad_maximum_fusion
  9.6 31.8 %all_to_all.58 = bf16[64,16,256]{2,1,0:T(8,128)(2,1)} all-to-all(bf16[64,16,256]{2,1,0:T(8,128)(2,1)S(1)} %bitcast.35), channel_id=1, replica_groups=mesh['y'=8,'xc'=8,'grp'=8] {'xc','grp'}, dimensions={0} | all-to-all | bytes 1048576 | tf_op jit(solution)/shard_map/all_to_all | solution.py:163
  41.4 1.1 copy.32
  42.5 4.3 %all-to-all-start = ((bf16[128,8,512]{2,0,1:T(8,128)(2,1)}), bf16[128,8,512]{2,0,1:T(8,128)(2,1)S(1)}, u32[]{:S(2)}, u32[]{:S(2)}) async-start(bf16[128,8,512]{2,0,1:T(8,128)(2,1)} %bitcast.30), calls=%async_computation | async-start | bytes 2097152 | tf_op jit(solution)/shard_map/all_to_all | solution.py:165
  46.8 1.1 copy.31
  47.9 28.2 %all-to-all-done = bf16[128,8,512]{2,0,1:T(8,128)(2,1)S(1)} async-done(((bf16[128,8,512]{2,0,1:T(8,128)(2,1)}), bf16[128,8,512]{2,0,1:T(8,128)(2,1)S(1)}, u32[]{:S(2)}, u32[]{:S(2)}) %all-to-all-start) | async-done | bytes 1048608 | tf_op jit(solution)/shard_map/all_to_all | solution.py:165
  76.1 3.6 %all-to-all-start.1 = ((bf16[128,8,512]{2,0,1:T(8,128)(2,1)}), bf16[128,8,512]{2,0,1:T(8,128)(2,1)S(1)}, u32[]{:S(2)}, u32[]{:S(2)}) async-start(bf16[128,8,512]{2,0,1:T(8,128)(2,1)} %bitcast.29), calls=%async_computation.1 | async-start | bytes 2097152 | tf_op jit(solution)/shard_map/all_to_all | solution.py:166
  79.6 0.1 copy.19
  79.8 0.2 reshape.36
  79.9 0.7 dynamic_slice.7.sel
  80.6 15.3 %all-gather.2.cloned.1.call-done.table = bf16[512,16,256]{2,1,0:T(8,128)(2,1)} async-done(((bf16[64,16,256]{2,1,0:T(8,128)(2,1)}), bf16[512,16,256]{2,1,0:T(8,128)(2,1)}) %all-gather.2.cloned.1.call-update) | async-done | bytes 4194320 | tf_op jit(solution)/shard_map/all_gather | solution.py:164
  95.9 5.1 %pack.1 = bf16[512,16,256]{2,1,0:T(8,128)(2,1)} custom-call(s32[512]{0:T(512)} %dynamic_slice.7.sel, bf16[512,16,256]{2,1,0:T(8,128)(2,1)} %all-gather.2.cloned.1.call-done.table), custom_call_target="tpu_custom_call" | custom-call | tf_op jit(solution)/shard_map/pack/pallas_call | solution.py:92
  101.0 7.8 %all-to-all-done.1 = bf16[128,8,512]{2,0,1:T(8,128)(2,1)S(1)} async-done(((bf16[128,8,512]{2,0,1:T(8,128)(2,1)}), bf16[128,8,512]{2,0,1:T(8,128)(2,1)S(1)}, u32[]{:S(2)}, u32[]{:S(2)}) %all-to-all-start.1) | async-done | bytes 1048608 | tf_op jit(solution)/shard_map/all_to_all | solution.py:166
  108.8 4.9 %all-to-all-start.3 = ((bf16[512,16,256]{2,1,0:T(8,128)(2,1)}), bf16[512,16,256]{2,1,0:T(8,128)(2,1)}, u32[]{:S(2)}, u32[]{:S(2)}) async-start(bf16[512,16,256]{2,1,0:T(8,128)(2,1)} %pack.1), calls=%async_computation.3 | async-start | bytes 8388608 | tf_op jit(solution)/shard_map/all_to_all | solution.py:168
  113.7 0.6 dynamic_slice.6.sel
  114.3 48.3 %all-to-all-done.3 = bf16[512,16,256]{2,1,0:T(8,128)(2,1)} async-done(((bf16[512,16,256]{2,1,0:T(8,128)(2,1)}), bf16[512,16,256]{2,1,0:T(8,128)(2,1)}, u32[]{:S(2)}, u32[]{:S(2)}) %all-to-all-start.3) | async-done | bytes 4194336 | tf_op jit(solution)/shard_map/all_to_all | solution.py:168
  162.6 23.0 %attention.1 = (bf16[1024,512]{1,0:T(8,128)(2,1)}, bf16[8,8,8,16,256]{4,3,2,1,0:T(8,128)(2,1)}) custom-call(s32[64]{0:T(128)} %dynamic_slice.6.sel, bf16[1024,512]{1,0:T(8,128)(2,1)} %bitcast.31, bf16[1024,512]{1,0:T(8,128)(2,1)} %bitcast.32, bf16[8,8,8,16,256]{4,3,2,1,0:T(8,128)(2,1)} %bitcast.6.kv_ref), custom_call_target="tpu_custom_call" | custom-call | tf_op jit(solution)/shard_map/attention/pallas_call | solution.py:124
  185.6 54.6 %all_to_all.59.rows = bf16[512,16,256]{2,1,0:T(8,128)(2,1)} all-to-all(bf16[512,16,256]{2,1,0:T(8,128)(2,1)} %bitcast.33), channel_id=1, replica_groups=mesh['y'=8,'xc'=8,'grp'=8] {'xc'}, dimensions={0} | all-to-all | bytes 8388608 | tf_op jit(solution)/shard_map/all_to_all | solution.py:171
  240.2 7.0 %accumulate.1 = bf16[512,16,256]{2,1,0:T(8,128)(2,1)} custom-call(s32[512]{0:T(512)} %dynamic_slice.7.sel, bf16[512,16,256]{2,1,0:T(8,128)(2,1)} %all_to_all.59.rows), custom_call_target="tpu_custom_call" | custom-call | tf_op jit(solution)/shard_map/accumulate/pallas_call | solution.py:106
  247.3 52.5 %reduce-scatter.2.cloned.1.call-done = bf16[64,16,256]{2,1,0:T(8,128)(2,1)} async-done(((bf16[512,16,256]{2,1,0:T(8,128)(2,1)}), bf16[64,16,256]{2,1,0:T(8,128)(2,1)}) %reduce-scatter.2.cloned.1.call-update) | async-done | bytes 524304 | tf_op jit(solution)/shard_map/reduce_scatter | solution.py:175
  299.7 14.2 %all_to_all.60 = bf16[64,16,256]{2,1,0:T(8,128)(2,1)S(1)} all-to-all(bf16[64,16,256]{2,1,0:T(8,128)(2,1)} %reduce-scatter.2.cloned.1.call-done), channel_id=1, replica_groups=mesh['y'=8,'xc'=8,'grp'=8] {'xc'}, dimensions={0} | all-to-all | bytes 1048576 | tf_op jit(solution)/shard_map/all_to_all | solution.py:176
  314.0 0.8 fusion
  (17 shorter events, 0.2 us)
Async XLA Ops:
  7.2 34.3 %copy-start.2 = (bf16[128,4096]{1,0:T(8,128)(2,1)S(1)}, bf16[128,4096]{1,0:T(8,128)(2,1)}, u32[]{:S(2)}) copy-start(bf16[128,4096]{1,0:T(8,128)(2,1)} %param.5) | copy-start | bytes 3145732
  7.2 88.8 %all-gather.2.cloned.1.call-start = ((), (), s32[]{:S(2)}) async-start(), calls=%async_computation.7 | async-start | bytes 4718592 | tf_op jit(solution)/shard_map/all_gather | solution.py:164
  8.3 38.5 %copy-start.3 = (bf16[128,4096]{1,0:T(8,128)(2,1)S(1)}, bf16[128,4096]{1,0:T(8,128)(2,1)}, u32[]{:S(2)}) copy-start(bf16[128,4096]{1,0:T(8,128)(2,1)} %param.8) | copy-start | bytes 3145732
  41.4 38.2 %copy-start.4 = (s32[512,1,8]{0,2,1:T(8,128)S(1)}, s32[512,1,8]{0,2,1:T(8,128)}, u32[]{:S(2)}) copy-start(s32[512,1,8]{0,2,1:T(8,128)} %param.9) | copy-start | bytes 49156
  42.5 33.5 %all-to-all-start = ((bf16[128,8,512]{2,0,1:T(8,128)(2,1)}), bf16[128,8,512]{2,0,1:T(8,128)(2,1)S(1)}, u32[]{:S(2)}, u32[]{:S(2)}) async-start(bf16[128,8,512]{2,0,1:T(8,128)(2,1)} %bitcast.30), calls=%async_computation | async-start | bytes 2097152 | tf_op jit(solution)/shard_map/all_to_all | solution.py:165
  76.1 24.9 %copy-start = (bf16[128,8,512]{2,0,1:T(8,128)(2,1)}, bf16[128,8,512]{2,0,1:T(8,128)(2,1)S(1)}, u32[]{:S(2)}) copy-start(bf16[128,8,512]{2,0,1:T(8,128)(2,1)S(1)} %all-to-all-done) | copy-start | bytes 3145732
  76.1 32.7 %all-to-all-start.1 = ((bf16[128,8,512]{2,0,1:T(8,128)(2,1)}), bf16[128,8,512]{2,0,1:T(8,128)(2,1)S(1)}, u32[]{:S(2)}, u32[]{:S(2)}) async-start(bf16[128,8,512]{2,0,1:T(8,128)(2,1)} %bitcast.29), calls=%async_computation.1 | async-start | bytes 2097152 | tf_op jit(solution)/shard_map/all_to_all | solution.py:166
  108.8 4.9 %copy-start.1 = (bf16[128,8,512]{2,0,1:T(8,128)(2,1)}, bf16[128,8,512]{2,0,1:T(8,128)(2,1)S(1)}, u32[]{:S(2)}) copy-start(bf16[128,8,512]{2,0,1:T(8,128)(2,1)S(1)} %all-to-all-done.1) | copy-start | bytes 3145732
  108.8 53.8 %all-to-all-start.3 = ((bf16[512,16,256]{2,1,0:T(8,128)(2,1)}), bf16[512,16,256]{2,1,0:T(8,128)(2,1)}, u32[]{:S(2)}, u32[]{:S(2)}) async-start(bf16[512,16,256]{2,1,0:T(8,128)(2,1)} %pack.1), calls=%async_computation.3 | async-start | bytes 8388608 | tf_op jit(solution)/shard_map/all_to_all | solution.py:168
  113.7 186.0 %reduce-scatter.2.cloned.1.call-start = ((), (), s32[]{:S(2)}) async-start(), calls=%async_computation.8 | async-start | bytes 4718592 | tf_op jit(solution)/shard_map/reduce_scatter | solution.py:175
Sparse Core Ops, SparseCore 0:
  41.5 54.3 all-gather.1
  247.4 52.2 reduce-scatter.1

commit v2 on v1

v2 whole, which is shorter than its diff:
```python
import functools

import jax
import jax.numpy as jnp
from jax import lax
from jax.experimental import pallas as pl
from jax.experimental.pallas import tpu as pltpu
from jax.sharding import PartitionSpec as P

HEAD_SIZE = 128
QUERY_HEADS = 32
KEY_HEADS = 8
BLOCK_TOKENS = 128
CHOSEN_BLOCKS = 8
GROUP = QUERY_HEADS // KEY_HEADS
PAIR = 2 * HEAD_SIZE
STRIPES = 8
ROWS = BLOCK_TOKENS // STRIPES
KEYS = CHOSEN_BLOCKS * BLOCK_TOKENS
FACTOR = HEAD_SIZE ** (-0.5)
VMEM = 56 * 1024 * 1024


def accumulate_kernel(sel, k_rows, v_rows, out, total):
    total[...] = jnp.zeros_like(total)

    @pl.loop(0, sel.shape[0], unroll=8)
    def _(r):
        total[sel[r], :, :HEAD_SIZE] += k_rows[r].astype(jnp.float32)
        total[sel[r], :, HEAD_SIZE:] += v_rows[r].astype(jnp.float32)

    out[...] = total[...].astype(out.dtype)


def nt(a, b):
    return lax.dot_general(a, b, (((1,), (1,)), ((), ())), preferred_element_type=jnp.float32)


def nn(a, b):
    return jnp.dot(a, b, preferred_element_type=jnp.float32)


def attention_block(i, own, sel_at, q_ref, g_ref, k_ref, v_ref, dq_ref, dk_ref, dv_ref, probs, dscores):
    rows = pl.ds(pl.multiple_of(i * BLOCK_TOKENS, BLOCK_TOKENS), BLOCK_TOKENS)
    units = pl.ds(pl.multiple_of(i * CHOSEN_BLOCKS, CHOSEN_BLOCKS), CHOSEN_BLOCKS)
    keys = k_ref[:, units].reshape(KEYS, HEAD_SIZE)
    vals = v_ref[:, units].reshape(KEYS, HEAD_SIZE)
    stripe = lax.broadcasted_iota(jnp.int32, (STRIPES, ROWS, BLOCK_TOKENS), 0)
    row = lax.broadcasted_iota(jnp.int32, (STRIPES, ROWS, BLOCK_TOKENS), 1)
    token = lax.broadcasted_iota(jnp.int32, (STRIPES, ROWS, BLOCK_TOKENS), 2)
    ahead = stripe * ROWS + row - token
    bias = jnp.stack(
        [
            jnp.where(ahead <= (own - sel_at(j)) * BLOCK_TOKENS, 0.0, -jnp.inf).astype(jnp.float32)
            for j in range(CHOSEN_BLOCKS)
        ],
        axis=1,
    ).reshape(KEYS, BLOCK_TOKENS)
    q_parts, g_parts = [], []
    for h in range(GROUP):
        cols = pl.ds(h * HEAD_SIZE, HEAD_SIZE)
        q, g = q_ref[i, :, cols], g_ref[i, :, cols]
        q_parts.append(q)
        g_parts.append(g)
        scores = nt(keys, q) * FACTOR + bias
        highest = jnp.max(scores, axis=0, keepdims=True)
        weights = jnp.exp(scores - highest)
        prob = weights * (1.0 / jnp.sum(weights, axis=0, keepdims=True))
        low = prob.astype(jnp.bfloat16)
        dprobs = nt(vals, g)
        delta = jnp.sum(low.astype(jnp.float32) * dprobs, axis=0, keepdims=True)
        probs[:, cols] = low
        dscores[:, cols] = (prob * (dprobs - delta)).astype(jnp.bfloat16)
    full = (STRIPES, CHOSEN_BLOCKS, ROWS, HEAD_SIZE)
    dv = nn(probs[...], jnp.concatenate(g_parts, 0))
    dv_ref[:, units] = dv.astype(jnp.bfloat16).reshape(full)
    dk = nn(dscores[...], jnp.concatenate(q_parts, 0)) * FACTOR
    dk_ref[:, units] = dk.astype(jnp.bfloat16).reshape(full)
    dq_t = nn(keys.T, dscores[...]) * FACTOR
    for h in range(GROUP):
        cols = pl.ds(h * HEAD_SIZE, HEAD_SIZE)
        dq_ref[rows, cols] = dq_t[:, h * HEAD_SIZE : (h + 1) * HEAD_SIZE].T.astype(jnp.bfloat16)


Y, C, Z = 8, 8, 8
UNITS = Z * CHOSEN_BLOCKS
SHARE = C * Z
HALF = SHARE // 2
STEPS = 4
SPLITS = 4
WIDE = GROUP * HEAD_SIZE


def at(index, size):
    return pl.ds(pl.multiple_of(index * size, size), size)


def front_kernel(
    sel, k, v, q, g, dq, ret_k_out, ret_v_out,
    kz, vz, qh, gh, tab_k, tab_v, out_k, out_v, in_k, in_v, dk_out, dv_out, ret_k, ret_v, probs, dscores,
    z_send, z_recv, s_send, s_recv, ag_send, ag_recv, k_send, k_recv, v_send, v_recv,
    rv_send, rv_recv, rk_send, rk_recv, own_sem,
):
    y, c, z = lax.axis_index("y"), lax.axis_index("xc"), lax.axis_index("grp")

    def device(dy=0, dc=0, dz=0):
        return (lax.rem(y + dy + Y, Y), lax.rem(c + dc, C), lax.rem(z + dz, Z))

    def remote(src, dst, send, recv, target):
        return pltpu.make_async_remote_copy(
            src_ref=src, dst_ref=dst, send_sem=send, recv_sem=recv,
            device_id=target, device_id_type=pl.DeviceIdType.MESH,
        )

    barrier = pltpu.get_barrier_semaphore()
    partners = [device(dz=d) for d in range(1, Z)] + [device(dc=d) for d in range(1, C)]
    partners += [device(dy=1), device(dy=-1)]
    for p in partners:
        pl.semaphore_signal(barrier, inc=1, device_id=p, device_id_type=pl.DeviceIdType.MESH)
    pl.semaphore_wait(barrier, len(partners))

    def z_copy(n, src, width, dst, d):
        to = lax.rem(z + d, Z)
        return remote(src.at[:, at(to, width)], dst.at[z], z_send.at[n, d], z_recv.at[n, d], device(dz=d))

    for d in range(1, Z):
        z_copy(0, k, HEAD_SIZE, kz, d).start()
        z_copy(1, v, HEAD_SIZE, vz, d).start()
    kz[z] = k[:, at(z, HEAD_SIZE)]
    vz[z] = v[:, at(z, HEAD_SIZE)]
    for d in range(1, Z):
        z_copy(0, k, HEAD_SIZE, kz, d).wait_recv()
        z_copy(1, v, HEAD_SIZE, vz, d).wait_recv()

    mine = pl.ds(pl.multiple_of(y * SHARE + c * Z, Z), Z)

    def s_copy(n, src, tab, d):
        to = lax.rem(c + d, C)
        return remote(src.at[:, at(to, ROWS)], tab.at[mine], s_send.at[n, d], s_recv.at[n, d], device(dc=d))

    for d in range(1, C):
        s_copy(0, kz, tab_k, d).start()
        s_copy(1, vz, tab_v, d).start()
    for d in range(1, Z):
        z_copy(2, q, WIDE, qh, d).start()
        z_copy(3, g, WIDE, gh, d).start()
    tab_k[mine] = kz[:, at(c, ROWS)]
    tab_v[mine] = vz[:, at(c, ROWS)]
    qh[z] = q[:, at(z, WIDE)]
    gh[z] = g[:, at(z, WIDE)]

    def ring(n, tab, s, way, half):
        owner = lax.rem(y - way * s + Y, Y)
        part = tab.at[pl.ds(pl.multiple_of(owner * SHARE + half * HALF, HALF), HALF)]
        lane = 0 if way > 0 else 1
        return remote(part, part, ag_send.at[n, s, lane, half], ag_recv.at[n, s, lane, half], device(dy=way))

    order = ((1, 0), (-1, 1), (1, 1), (-1, 0))

    def ring_first(n, tab):
        for way, half in order:
            ring(n, tab, 0, way, half).start()

    def ring_next(n, tab, s):
        for way, half in order[: 2 if s == STEPS - 1 else 4]:
            ring(n, tab, s - 1, way, half).wait_recv()
            ring(n, tab, s, way, half).start()

    def ring_last(n, tab):
        for way, half in order[2:]:
            ring(n, tab, STEPS - 2, way, half).wait_recv()
        for way, half in order[:2]:
            ring(n, tab, STEPS - 1, way, half).wait_recv()

    def pack(tab, out, own, first, count):
        for d in range(C):
            to = lax.rem(c + d, C)

            @pl.loop(0, count, unroll=8)
            def _(u):
                rows = tab[sel[to * UNITS + first + u]]
                if d:
                    out[d, first + u] = rows
                else:
                    own[c, first + u] = rows

    def k_copy(d):
        return remote(out_k.at[d], in_k.at[c], k_send.at[d], k_recv.at[d], device(dc=d))

    part = UNITS // SPLITS

    def v_copy(d, n):
        return remote(
            out_v.at[d, at(n, part)], in_v.at[c, at(n, part)], v_send.at[d, n], v_recv.at[d, n], device(dc=d)
        )

    def rv_copy(d, n):
        to = lax.rem(c + d, C)
        return remote(
            dv_out.at[to, at(n, part)], ret_v.at[c, at(n, part)], rv_send.at[d, n], rv_recv.at[d, n], device(dc=d)
        )

    def rk_copy(d):
        to = lax.rem(c + d, C)
        return remote(dk_out.at[to], ret_k.at[c], rk_send.at[d], rk_recv.at[d], device(dc=d))

    for d in range(1, C):
        s_copy(0, kz, tab_k, d).wait_recv()
    ring_first(0, tab_k)
    for d in range(1, C):
        s_copy(1, vz, tab_v, d).wait_recv()
    for s in range(1, STEPS):
        ring_next(0, tab_k, s)
    ring_first(1, tab_v)
    ring_last(0, tab_k)
    pack(tab_k, out_k, in_k, 0, UNITS)
    for d in range(1, C):
        k_copy(d).start()
    for s in range(1, STEPS):
        ring_next(1, tab_v, s)
    ring_last(1, tab_v)

    for n in range(SPLITS):
        pack(tab_v, out_v, in_v, n * part, part)
        for d in range(1, C):
            v_copy(d, n).start()

    for d in range(1, Z):
        z_copy(2, q, WIDE, qh, d).wait_recv()
        z_copy(3, g, WIDE, gh, d).wait_recv()
    for d in range(1, C):
        k_copy(d).wait_recv()

    @pl.loop(0, SPLITS)
    def _(n):
        for d in range(1, C):
            v_copy(d, n).wait_recv()

        @pl.loop(0, Z // SPLITS)
        def _(m):
            i = n * (Z // SPLITS) + m
            first = c * UNITS + i * CHOSEN_BLOCKS
            attention_block(
                i, sel[first], lambda j: sel[first + j],
                qh, gh, in_k, in_v, dq, dk_out, dv_out, probs, dscores,
            )

        for d in range(1, C):
            rv_copy(d, n).start()

    for d in range(1, C):
        rk_copy(d).start()
    own_v = pltpu.make_async_copy(dv_out.at[c], ret_v.at[c], own_sem.at[0])
    own_k = pltpu.make_async_copy(dk_out.at[c], ret_k.at[c], own_sem.at[1])
    own_v.start()
    own_k.start()
    own_v.wait()
    own_k.wait()
    for d in range(1, C):
        for n in range(SPLITS):
            rv_copy(d, n).wait_recv()
    for d in range(1, C):
        rk_copy(d).wait_recv()
    ret_k_out[...] = ret_k[...]
    ret_v_out[...] = ret_v[...]

    for d in range(1, Z):
        for n, (src, width, dst) in enumerate(
            ((k, HEAD_SIZE, kz), (v, HEAD_SIZE, vz), (q, WIDE, qh), (g, WIDE, gh))
        ):
            z_copy(n, src, width, dst, d).wait_send()
    for d in range(1, C):
        s_copy(0, kz, tab_k, d).wait_send()
        s_copy(1, vz, tab_v, d).wait_send()
        k_copy(d).wait_send()
        rk_copy(d).wait_send()
        for n in range(SPLITS):
            v_copy(d, n).wait_send()
            rv_copy(d, n).wait_send()
    for n, tab in ((0, tab_k), (1, tab_v)):
        for s in range(STEPS):
            for way, half in order[: 2 if s == STEPS - 1 else 4]:
                ring(n, tab, s, way, half).wait_send()


def front(sel, k, v, q, g):
    vmem = pl.BlockSpec(memory_space=pltpu.VMEM)
    bf16 = lambda *shape: pltpu.VMEM(shape, jnp.bfloat16)
    dma = lambda *shape: pltpu.SemaphoreType.DMA(shape)
    units = (C, UNITS, ROWS, HEAD_SIZE)
    table = (Y * SHARE, ROWS, HEAD_SIZE)
    return pl.pallas_call(
        front_kernel,
        out_shape=(
            jax.ShapeDtypeStruct((Z * BLOCK_TOKENS, WIDE), jnp.bfloat16),
            jax.ShapeDtypeStruct(units, jnp.bfloat16),
            jax.ShapeDtypeStruct(units, jnp.bfloat16),
        ),
        in_specs=[pl.BlockSpec(memory_space=pltpu.SMEM)] + [vmem] * 4,
        out_specs=[vmem] * 3,
        scratch_shapes=[bf16(Z, BLOCK_TOKENS, HEAD_SIZE)] * 2
        + [bf16(Z, BLOCK_TOKENS, WIDE)] * 2
        + [bf16(*table)] * 2
        + [bf16(*units)] * 8
        + [bf16(KEYS, WIDE)] * 2
        + [dma(4, Z)] * 2
        + [dma(2, C)] * 2
        + [dma(2, STEPS, 2, 2)] * 2
        + [dma(C)] * 2
        + [dma(C, SPLITS)] * 2
        + [dma(C, SPLITS)] * 2
        + [dma(C)] * 2
        + [dma(2)],
        compiler_params=pltpu.CompilerParams(
            vmem_limit_bytes=VMEM, collective_id=0, has_side_effects=True
        ),
        name="front",
    )(sel, k, v, q, g)


def accumulate(sel, k_rows, v_rows, blocks):
    shape = (blocks, ROWS, PAIR)
    return pl.pallas_call(
        accumulate_kernel,
        out_shape=jax.ShapeDtypeStruct(shape, jnp.bfloat16),
        in_specs=[
            pl.BlockSpec(memory_space=pltpu.SMEM),
            pl.BlockSpec(memory_space=pltpu.VMEM),
            pl.BlockSpec(memory_space=pltpu.VMEM),
        ],
        out_specs=pl.BlockSpec(memory_space=pltpu.VMEM),
        scratch_shapes=[pltpu.VMEM(shape, jnp.float32)],
        compiler_params=pltpu.CompilerParams(vmem_limit_bytes=VMEM),
        name="accumulate",
    )(sel, k_rows, v_rows)


def body(query, keys, values, output_cotangent, select):
    row = lax.axis_index("y")
    flat = select.reshape(Y * SHARE * CHOSEN_BLOCKS)
    width = C * UNITS
    row_select = lax.dynamic_slice_in_dim(flat, row * width, width, 0)
    grad_query, ret_k, ret_v = front(row_select, keys, values, query, output_cotangent)
    rows = (width, ROWS, HEAD_SIZE)
    sums = accumulate(row_select, ret_k.reshape(rows), ret_v.reshape(rows), Y * SHARE)
    row_sums = lax.psum_scatter(sums, "y", scatter_dimension=0, tiled=True)
    own = lax.all_to_all(row_sums, "xc", split_axis=0, concat_axis=0, tiled=True)
    own = jnp.transpose(own.reshape(C, Z, ROWS, PAIR), (1, 0, 2, 3))
    own = own.reshape(Z * BLOCK_TOKENS, PAIR)
    return grad_query, own[:, :HEAD_SIZE], own[:, HEAD_SIZE:]


def solution(mesh):
    groups = mesh.shape["grp"]
    grid = jax.sharding.Mesh(
        mesh.devices.reshape(-1, STRIPES, groups), ("y", "xc", "grp")
    )
    rows = ("y", "xc")
    in_specs = (P(rows + ("grp",), None),) * 4 + (P(None, "grp", None),)
    out_specs = (P(rows, "grp"),) * 3
    return jax.shard_map(
        body, mesh=grid, in_specs=in_specs, out_specs=out_specs, check_vma=False
    )
```

time: 322 us -> 251 us (0.78)
  Pallas kernels: 35 us -> 165 us
  blocking collectives: 101 us -> 0 us
  waiting for transfers between devices: 152 us -> 63 us
  starting transfers between devices: 12.8 us -> 4.93 us
  local copies, waits for them, and re-layouts: 6.78 us -> 3.48 us
    pallas_call x3 -> x2, Pallas kernels: 35 us -> 165 us  [the longest x1 156 us: front(): pl.pallas_call(front_kernel, out_shape=(jax.ShapeDtypeStruct((Z * BLOCK_T...]
    all_to_all x3 -> x0, blocking collectives: 101 us -> none  [the longest x1 54.6 us: body(): lax.all_to_all(unit_grads.reshape(width, ROWS, PAIR), 'xc', split_axis=0,...]
    all_to_all x3 -> x1, waiting for transfers between devices: 84.3 us -> 9.48 us  [body(): lax.all_to_all(row_sums, 'xc', split_axis=0, concat_axis=0, tiled=True)]
    all_gather x1 -> x0, waiting for transfers between devices: 15.3 us -> none  [body(): table = lax.all_gather(share, 'y', axis=0, tiled=True)]
    all_to_all x3 -> x1, starting transfers between devices: 12.8 us -> 4.89 us  [body(): lax.all_to_all(row_sums, 'xc', split_axis=0, concat_axis=0, tiled=True)]
  transfers between devices with their start and end apart: 5 -> 2, of which waited for: 5 -> 2; matrix products, arithmetic and copies ran while one was open for 1% -> 0% of each run, Pallas kernels for 2% -> 0%
where the time goes in v2:
time: 251 us
  Pallas kernels  165 us (66%)
  waiting for transfers between devices  63 us (25%)
  between operations  14.1 us (6%)
  starting transfers between devices  4.93 us (2%)
  local copies, waits for them, and re-layouts  3.48 us (1%)
    pallas_call x1, Pallas kernels, front(): pl.pallas_call(front_kernel, out_shape=(jax.ShapeDtypeStruct((Z * BLOCK_T...  156 us
    reduce_scatter x1, waiting for transfers between devices, body(): row_sums = lax.psum_scatter(sums, 'y', scatter_dimension=0, tiled=True)  53.5 us
    all_to_all x1, waiting for transfers between devices, body(): lax.all_to_all(row_sums, 'xc', split_axis=0, concat_axis=0, tiled=True)  9.48 us
    pallas_call x1, Pallas kernels, accumulate(): pl.pallas_call(accumulate_kernel, out_shape=jax.ShapeDtypeStruct(shape, j...  8.62 us
  transfers between devices with their start and end apart: 2, of which 2 were waited for; matrix products, arithmetic and copies ran while one was open for 0% of the time, Pallas kernels for 0%

profile of v2, /device:TPU:1, one launch (start us, length us, event | category | flops | bytes accessed | tf_op | source)
XLA Modules:
  0.0 250.5 jit_solution(13665595056754544650)
XLA Ops:
  7.2 0.0 reduce-scatter.2.cloned.1.call-start
  7.2 0.8 copy.9
  8.1 0.1 reshape.21
  8.2 0.7 dynamic_slice.3.sel
  8.9 156.5 %front.1 = (bf16[1024,512]{1,0:T(8,128)(2,1)}, bf16[8,64,16,128]{3,2,1,0:T(8,128)(2,1)}, bf16[8,64,16,128]{3,2,1,0:T(8,128)(2,1)}) custom-call(s32[512]{0:T(512)} %dynamic_slice.3.sel, bf16[128,1024]{1,0:T(8,128)(2,1)} %k.1, bf16[128,1024]{1,0:T(8,128)(2,1)} %v.1, bf16[128,4096]{1,0:T(8,128)(2,1)} %q.1, bf16[128,4096]{1,0:T(8,128)(2,1)} %g.1), custom_call_target="tpu_custom_call" | custom-call | tf_op jit(solution)/shard_map/front/pallas_call | solution.py:292
  165.3 8.6 %accumulate.1 = bf16[512,16,256]{2,1,0:T(8,128)(2,1)} custom-call(s32[512]{0:T(512)} %dynamic_slice.3.sel, bf16[512,16,128]{2,1,0:T(8,128)(2,1)} %bitcast.8, bf16[512,16,128]{2,1,0:T(8,128)(2,1)} %bitcast.9), custom_call_target="tpu_custom_call" | custom-call | tf_op jit(solution)/shard_map/accumulate/pallas_call | solution.py:323
  174.0 0.0 reduce-scatter.2.cloned.1.call-update
  174.0 0.0 copy-start
  174.0 53.5 %reduce-scatter.2.cloned.1.call-done = bf16[64,16,256]{2,1,0:T(8,128)(2,1)} async-done(((bf16[512,16,256]{2,1,0:T(8,128)(2,1)}), bf16[64,16,256]{2,1,0:T(8,128)(2,1)}) %reduce-scatter.2.cloned.1.call-update) | async-done | bytes 524304 | tf_op jit(solution)/shard_map/reduce_scatter | solution.py:346
  227.5 4.9 %all-to-all-start = ((bf16[64,16,256]{2,1,0:T(8,128)(2,1)}), bf16[64,16,256]{2,1,0:T(8,128)(2,1)S(1)}, u32[]{:S(2)}, u32[]{:S(2)}) async-start(bf16[64,16,256]{2,1,0:T(8,128)(2,1)} %reduce-scatter.2.cloned.1.call-done), calls=%async_computation.1 | async-start | bytes 1048576 | tf_op jit(solution)/shard_map/all_to_all | solution.py:347
  232.4 9.5 %all-to-all-done = bf16[64,16,256]{2,1,0:T(8,128)(2,1)S(1)} async-done(((bf16[64,16,256]{2,1,0:T(8,128)(2,1)}), bf16[64,16,256]{2,1,0:T(8,128)(2,1)S(1)}, u32[]{:S(2)}, u32[]{:S(2)}) %all-to-all-start) | async-done | bytes 524320 | tf_op jit(solution)/shard_map/all_to_all | solution.py:347
  241.9 0.8 fusion
  242.7 0.0 copy-done
  242.7 1.0 copy.12
  (1 shorter events, 0.0 us)
Async XLA Ops:
  7.2 220.3 %reduce-scatter.2.cloned.1.call-start = ((), (), s32[]{:S(2)}) async-start(), calls=%async_computation.2 | async-start | bytes 4718592 | tf_op jit(solution)/shard_map/reduce_scatter | solution.py:346
  174.0 68.7 %copy-start = (bf16[1024,512]{1,0:T(8,128)(2,1)S(1)}, bf16[1024,512]{1,0:T(8,128)(2,1)}, u32[]{:S(2)}) copy-start(bf16[1024,512]{1,0:T(8,128)(2,1)} %get-tuple-element.14) | copy-start | bytes 3145732
  227.5 14.4 %all-to-all-start = ((bf16[64,16,256]{2,1,0:T(8,128)(2,1)}), bf16[64,16,256]{2,1,0:T(8,128)(2,1)S(1)}, u32[]{:S(2)}, u32[]{:S(2)}) async-start(bf16[64,16,256]{2,1,0:T(8,128)(2,1)} %reduce-scatter.2.cloned.1.call-done), calls=%async_computation.1 | async-start | bytes 1048576 | tf_op jit(solution)/shard_map/all_to_all | solution.py:347
Sparse Core Ops, SparseCore 0:
  174.1 53.3 reduce-scatter.1

commit v3 on v2

v3 whole, which is shorter than its diff:
```python
import functools

import jax
import jax.numpy as jnp
from jax import lax
from jax.experimental import pallas as pl
from jax.experimental.pallas import tpu as pltpu
from jax.sharding import PartitionSpec as P

HEAD_SIZE = 128
QUERY_HEADS = 32
KEY_HEADS = 8
BLOCK_TOKENS = 128
CHOSEN_BLOCKS = 8
GROUP = QUERY_HEADS // KEY_HEADS
STRIPES = 8
ROWS = BLOCK_TOKENS // STRIPES
KEYS = CHOSEN_BLOCKS * BLOCK_TOKENS
FACTOR = HEAD_SIZE ** (-0.5)
VMEM = 56 * 1024 * 1024


def nt(a, b):
    return lax.dot_general(a, b, (((1,), (1,)), ((), ())), preferred_element_type=jnp.float32)


def nn(a, b):
    return jnp.dot(a, b, preferred_element_type=jnp.float32)


Y, C, Z = 8, 8, 8
OTHERS = CHOSEN_BLOCKS - 1
OTHER_KEYS = OTHERS * BLOCK_TOKENS
UNITS = Z * OTHERS
REQUESTS = C * UNITS
SLOTS = C * Z * CHOSEN_BLOCKS
SHARE = C * Z
BLOCKS = Y * SHARE
HALF = SHARE // 2
STEPS = 4
SPLITS = 4
PER_SPLIT = Z // SPLITS
WIDE = GROUP * HEAD_SIZE


def at(index, size):
    return pl.ds(pl.multiple_of(index * size, size), size)


def attention_block(
    i, own, sel_at, q_ref, g_ref, kz, vz, k_ref, v_ref, dq_ref, dk_own, dv_own, dk_ref, dv_ref, probs, dscores
):
    units = pl.ds(i * OTHERS, OTHERS)
    keys = jnp.concatenate([kz[i], k_ref[:, units].reshape(OTHER_KEYS, HEAD_SIZE)], 0)
    vals = jnp.concatenate([vz[i], v_ref[:, units].reshape(OTHER_KEYS, HEAD_SIZE)], 0)
    row = lax.broadcasted_iota(jnp.int32, (BLOCK_TOKENS, BLOCK_TOKENS), 0)
    token = lax.broadcasted_iota(jnp.int32, (BLOCK_TOKENS, BLOCK_TOKENS), 1)
    own_bias = jnp.where(row <= token, 0.0, -jnp.inf).astype(jnp.float32)
    other_bias = jnp.stack(
        [
            jnp.full(
                (STRIPES, ROWS, BLOCK_TOKENS), jnp.where(sel_at(j) < own, 0.0, -jnp.inf), jnp.float32
            )
            for j in range(1, CHOSEN_BLOCKS)
        ],
        axis=1,
    ).reshape(OTHER_KEYS, BLOCK_TOKENS)
    bias = jnp.concatenate([own_bias, other_bias], 0)
    q_parts, g_parts = [], []
    for h in range(GROUP):
        cols = pl.ds(h * HEAD_SIZE, HEAD_SIZE)
        q, g = q_ref[i, :, cols], g_ref[i, :, cols]
        q_parts.append(q)
        g_parts.append(g)
        scores = nt(keys, q) * FACTOR + bias
        highest = jnp.max(scores, axis=0, keepdims=True)
        weights = jnp.exp(scores - highest)
        prob = weights * (1.0 / jnp.sum(weights, axis=0, keepdims=True))
        low = prob.astype(jnp.bfloat16)
        dprobs = nt(vals, g)
        delta = jnp.sum(low.astype(jnp.float32) * dprobs, axis=0, keepdims=True)
        probs[:, cols] = low
        dscores[:, cols] = (prob * (dprobs - delta)).astype(jnp.bfloat16)
    others = (STRIPES, OTHERS, ROWS, HEAD_SIZE)
    dv = nn(probs[...], jnp.concatenate(g_parts, 0))
    dv_own[i] = dv[:BLOCK_TOKENS]
    dv_ref[:, units] = dv[BLOCK_TOKENS:].astype(jnp.bfloat16).reshape(others)
    dk = nn(dscores[...], jnp.concatenate(q_parts, 0)) * FACTOR
    dk_own[i] = dk[:BLOCK_TOKENS]
    dk_ref[:, units] = dk[BLOCK_TOKENS:].astype(jnp.bfloat16).reshape(others)
    dq_t = nn(keys.T, dscores[...]) * FACTOR
    for h in range(GROUP):
        cols = pl.ds(h * HEAD_SIZE, HEAD_SIZE)
        dq_ref[at(i, BLOCK_TOKENS), cols] = (
            dq_t[:, h * HEAD_SIZE : (h + 1) * HEAD_SIZE].T.astype(jnp.bfloat16)
        )


def order_requests(sel_row, order):
    lane = lax.broadcasted_iota(jnp.int32, (1, SLOTS), 1)
    key = jnp.where(lax.rem(lane, CHOSEN_BLOCKS) == 0, BLOCKS * SLOTS, sel_row * SLOTS + lane)

    def column(x):
        return jnp.broadcast_to(x, (128, SLOTS)).T[:, :1]

    index = lax.broadcasted_iota(jnp.int32, (SLOTS, 1), 0)
    valid = lax.rem(index, CHOSEN_BLOCKS) != 0
    chosen = column(sel_row)
    rank = jnp.sum((key < column(key)).astype(jnp.int32), axis=1, keepdims=True)
    rank = jnp.where(valid, rank, -2)
    place = lax.div(index, CHOSEN_BLOCKS) * OTHERS + lax.rem(index, CHOSEN_BLOCKS) - 1

    def pick(mask, value):
        return jnp.sum(jnp.where(mask, value, 0), axis=0, keepdims=True)

    here = pick(rank == lane, chosen + 1)
    before = pick(rank + 1 == lane, chosen + 1)
    upto = pick(valid & (chosen <= lane), 1)
    count = pick(valid & (chosen == lane), 1)
    order[...] = jnp.zeros_like(order)
    order[0:1, :] = pick(rank == lane, place)
    order[1:2, :] = (here == before).astype(jnp.int32)
    order[2:3, :] = jnp.where(count > 0, upto - 1, REQUESTS)


def whole_kernel(
    sel, sel_row, k, v, q, g, dq, dk, dv,
    kz, vz, qh, gh, tab_k, tab_v, out_k, out_v, in_k, in_v, dk_out, dv_out, ret_k, ret_v, probs, dscores,
    dk_own, dv_own, runs, rs_out, rs_in, fin_out, fin_in, order_v, order,
    z_send, z_recv, s_send, s_recv, ag_send, ag_recv, k_send, k_recv, v_send, v_recv,
    rv_send, rv_recv, rk_send, rk_recv, rs_send, rs_recv, u_send, u_recv, own_sem,
):
    y, c, z = lax.axis_index("y"), lax.axis_index("xc"), lax.axis_index("grp")

    def device(dy=0, dc=0, dz=0):
        return (lax.rem(y + dy + Y, Y), lax.rem(c + dc, C), lax.rem(z + dz, Z))

    def remote(src, dst, send, recv, target):
        return pltpu.make_async_remote_copy(
            src_ref=src, dst_ref=dst, send_sem=send, recv_sem=recv,
            device_id=target, device_id_type=pl.DeviceIdType.MESH,
        )

    barrier = pltpu.get_barrier_semaphore()
    partners = [device(dz=d) for d in range(1, Z)] + [device(dc=d) for d in range(1, C)]
    partners += [device(dy=1), device(dy=-1)]
    for p in partners:
        pl.semaphore_signal(barrier, inc=1, device_id=p, device_id_type=pl.DeviceIdType.MESH)
    pl.semaphore_wait(barrier, len(partners))

    by_head = ((k, HEAD_SIZE, kz), (v, HEAD_SIZE, vz), (q, WIDE, qh), (g, WIDE, gh))

    def z_copy(n, d):
        src, width, dst = by_head[n]
        to = lax.rem(z + d, Z)
        return remote(src.at[:, at(to, width)], dst.at[z], z_send.at[n, d], z_recv.at[n, d], device(dz=d))

    for n in range(2):
        for d in range(1, Z):
            z_copy(n, d).start()
    for src, width, dst in by_head:
        dst[z] = src[:, at(z, width)]

    mine = at(y * C + c, Z)
    to_table = ((kz, tab_k), (vz, tab_v))

    def s_copy(n, d):
        src, tab = to_table[n]
        to = lax.rem(c + d, C)
        return remote(src.at[:, at(to, ROWS)], tab.at[mine], s_send.at[n, d], s_recv.at[n, d], device(dc=d))

    for n in range(2):
        for d in range(1, Z):
            z_copy(n, d).wait_recv()
        for d in range(1, C):
            s_copy(n, d).start()
        src, tab = to_table[n]
        tab[mine] = src[:, at(c, ROWS)]
    for n in (2, 3):
        for d in range(1, Z):
            z_copy(n, d).start()

    def ring(n, s, way, half):
        tab = to_table[n][1]
        owner = lax.rem(y - way * s + Y, Y)
        part = tab.at[at(owner * 2 + half, HALF)]
        lane = 0 if way > 0 else 1
        return remote(part, part, ag_send.at[n, s, lane, half], ag_recv.at[n, s, lane, half], device(dy=way))

    ring_order = ((1, 0), (-1, 1), (1, 1), (-1, 0))

    def ring_first(n):
        for way, half in ring_order:
            ring(n, 0, way, half).start()

    def ring_next(n, s):
        for way, half in ring_order[: 2 if s == STEPS - 1 else 4]:
            ring(n, s - 1, way, half).wait_recv()
            ring(n, s, way, half).start()

    def ring_last(n):
        for way, half in ring_order[2:]:
            ring(n, STEPS - 2, way, half).wait_recv()
        for way, half in ring_order[:2]:
            ring(n, STEPS - 1, way, half).wait_recv()

    def pack(tab, out, own, first, count):
        for d in range(C):
            to = lax.rem(c + d, C)

            @pl.loop(first, first + count)
            def _(i):
                for j in range(OTHERS):
                    rows = tab[sel[(to * Z + i) * CHOSEN_BLOCKS + 1 + j]]
                    if d:
                        out[d, i * OTHERS + j] = rows
                    else:
                        own[c, i * OTHERS + j] = rows

    def k_copy(d):
        return remote(out_k.at[d], in_k.at[c], k_send.at[d], k_recv.at[d], device(dc=d))

    part = UNITS // SPLITS

    def v_copy(d, n):
        span = pl.ds(n * part, part)
        return remote(out_v.at[d, span], in_v.at[c, span], v_send.at[d, n], v_recv.at[d, n], device(dc=d))

    def rv_copy(d, n):
        to = lax.rem(c + d, C)
        return remote(
            dv_out.at[to, pl.ds(n * part, part)], ret_v.at[pl.ds(c * UNITS + n * part, part)],
            rv_send.at[d, n], rv_recv.at[d, n], device(dc=d),
        )

    def rk_copy(d):
        to = lax.rem(c + d, C)
        return remote(dk_out.at[to], ret_k.at[at(c, UNITS)], rk_send.at[d], rk_recv.at[d], device(dc=d))

    for d in range(1, C):
        s_copy(0, d).wait_recv()
    ring_first(0)
    for d in range(1, C):
        s_copy(1, d).wait_recv()
    for s in range(1, STEPS):
        ring_next(0, s)
    ring_first(1)
    ring_last(0)
    pack(tab_k, out_k, in_k, 0, Z)
    for d in range(1, C):
        k_copy(d).start()
    for s in range(1, STEPS):
        ring_next(1, s)
    order_requests(sel_row[...], order_v)
    to_scalars = pltpu.make_async_copy(order_v, order, own_sem.at[2])
    to_scalars.start()
    to_scalars.wait()
    ring_last(1)

    for n in range(SPLITS):
        pack(tab_v, out_v, in_v, n * PER_SPLIT, PER_SPLIT)
        for d in range(1, C):
            v_copy(d, n).start()

    for n in (2, 3):
        for d in range(1, Z):
            z_copy(n, d).wait_recv()
    for d in range(1, C):
        k_copy(d).wait_recv()

    @pl.loop(0, SPLITS)
    def _(n):
        for d in range(1, C):
            v_copy(d, n).wait_recv()

        @pl.loop(0, PER_SPLIT)
        def _(m):
            i = n * PER_SPLIT + m
            first = (c * Z + i) * CHOSEN_BLOCKS
            attention_block(
                i, sel[first], lambda j: sel[first + j],
                qh, gh, kz, vz, in_k, in_v, dq, dk_own, dv_own, dk_out, dv_out, probs, dscores,
            )

        for d in range(1, C):
            rv_copy(d, n).start()

    for d in range(1, C):
        rk_copy(d).start()
    own_v = pltpu.make_async_copy(dv_out.at[c], ret_v.at[at(c, UNITS)], own_sem.at[0])
    own_k = pltpu.make_async_copy(dk_out.at[c], ret_k.at[at(c, UNITS)], own_sem.at[1])
    own_v.start()
    own_k.start()
    own_v.wait()
    own_k.wait()

    nothing = jnp.zeros((ROWS, HEAD_SIZE), jnp.float32)
    runs[REQUESTS] = nothing

    def run_sums(ret):
        def add(p, total):
            total = ret[order[0, p]].astype(jnp.float32) + jnp.where(order[1, p] == 1, total, 0.0)
            runs[p] = total
            return total

        lax.fori_loop(0, REQUESTS, add, nothing, unroll=8)

    def rs_copy(n, s, way, half):
        lane = 0 if way > 0 else 1
        return remote(
            rs_out.at[n, lane, s, half], rs_in.at[n, lane, s, half],
            rs_send.at[n, lane, s, half], rs_recv.at[n, lane, s, half], device(dy=way),
        )

    def rs_step(n, s, way, half, arrived):
        lane = 0 if way > 0 else 1
        owner = lax.rem(y + way * (STEPS - s) + Y, Y)
        if arrived:
            rs_copy(n, s - 1, way, half).wait_recv()

        @pl.loop(0, HALF, unroll=8)
        def _(t):
            total = runs[order[2, owner * SHARE + half * HALF + t]]
            if arrived:
                total += rs_in[n, lane, s - 1, half, t].astype(jnp.float32)
            rs_out[n, lane, s, half, t] = total.astype(jnp.bfloat16)

        rs_copy(n, s, way, half).start()

    def u_copy(n, d):
        to = lax.rem(c + d, C)
        return remote(
            fin_out.at[n, at(to, Z)], fin_in.at[n, :, at(c, ROWS)], u_send.at[n, d], u_recv.at[n, d], device(dc=d)
        )

    def reduce(n):
        for way, half in ring_order[:2]:
            rs_step(n, 0, way, half, False)
        for way, half in ring_order[2:]:
            rs_step(n, 1, way, half, False)
        for way, half in ring_order[:2]:
            rs_step(n, 1, way, half, True)
        for s in range(2, STEPS):
            for way, half in ring_order[2:] + ring_order[:2]:
                rs_step(n, s, way, half, True)
        for half in (1, 0):
            for way in (1, -1):
                rs_copy(n, STEPS - 1, way, half).wait_recv()

            @pl.loop(0, HALF, unroll=8)
            def _(t):
                total = runs[order[2, y * SHARE + half * HALF + t]]
                for lane in range(2):
                    total += rs_in[n, lane, STEPS - 1, half, t].astype(jnp.float32)
                fin_out[n, half * HALF + t] = total.astype(jnp.bfloat16)

        for d in range(1, C):
            u_copy(n, d).start()
        fin_in[n, :, at(c, ROWS)] = fin_out[n, at(c, Z)]

    for n in range(SPLITS):
        for d in range(1, C):
            rv_copy(d, n).wait_recv()
    run_sums(ret_v)
    reduce(1)
    for d in range(1, C):
        rk_copy(d).wait_recv()
    run_sums(ret_k)
    reduce(0)
    for n, own, out in ((1, dv_own, dv), (0, dk_own, dk)):
        for d in range(1, C):
            u_copy(n, d).wait_recv()
        for i in range(Z):
            out[i] = (fin_in[n, i].astype(jnp.float32) + own[i]).astype(jnp.bfloat16)

    for d in range(1, Z):
        for n in range(4):
            z_copy(n, d).wait_send()
    for d in range(1, C):
        for n in range(2):
            s_copy(n, d).wait_send()
            u_copy(n, d).wait_send()
        k_copy(d).wait_send()
        rk_copy(d).wait_send()
        for n in range(SPLITS):
            v_copy(d, n).wait_send()
            rv_copy(d, n).wait_send()
    for n in range(2):
        for s in range(STEPS):
            for way, half in ring_order[: 2 if s == STEPS - 1 else 4]:
                ring(n, s, way, half).wait_send()
            for way, half in ring_order[: 2 if s == 0 else 4]:
                rs_copy(n, s, way, half).wait_send()


def whole(sel, k, v, q, g):
    vmem = pl.BlockSpec(memory_space=pltpu.VMEM)
    bf16 = lambda *shape: pltpu.VMEM(shape, jnp.bfloat16)
    f32 = lambda *shape: pltpu.VMEM(shape, jnp.float32)
    dma = lambda *shape: pltpu.SemaphoreType.DMA(shape)
    units = (C, UNITS, ROWS, HEAD_SIZE)
    table = (BLOCKS, ROWS, HEAD_SIZE)
    heads = (Z, BLOCK_TOKENS, HEAD_SIZE)
    steps = (2, 2, STEPS, 2, HALF, ROWS, HEAD_SIZE)
    return pl.pallas_call(
        whole_kernel,
        out_shape=(
            jax.ShapeDtypeStruct((Z * BLOCK_TOKENS, WIDE), jnp.bfloat16),
            jax.ShapeDtypeStruct(heads, jnp.bfloat16),
            jax.ShapeDtypeStruct(heads, jnp.bfloat16),
        ),
        in_specs=[pl.BlockSpec(memory_space=pltpu.SMEM)] + [vmem] * 5,
        out_specs=[vmem] * 3,
        scratch_shapes=[bf16(*heads)] * 2
        + [bf16(Z, BLOCK_TOKENS, WIDE)] * 2
        + [bf16(*table)] * 2
        + [bf16(*units)] * 6
        + [bf16(REQUESTS, ROWS, HEAD_SIZE)] * 2
        + [bf16(KEYS, WIDE)] * 2
        + [f32(*heads)] * 2
        + [f32(REQUESTS + 8, ROWS, HEAD_SIZE)]
        + [bf16(*steps)] * 2
        + [bf16(2, SHARE, ROWS, HEAD_SIZE)]
        + [bf16(2, *heads)]
        + [pltpu.VMEM((8, SLOTS), jnp.int32), pltpu.SMEM((8, SLOTS), jnp.int32)]
        + [dma(4, Z)] * 2
        + [dma(2, C)] * 2
        + [dma(2, STEPS, 2, 2)] * 2
        + [dma(C)] * 2
        + [dma(C, SPLITS)] * 2
        + [dma(C, SPLITS)] * 2
        + [dma(C)] * 2
        + [dma(2, 2, STEPS, 2)] * 2
        + [dma(2, C)] * 2
        + [dma(3)],
        compiler_params=pltpu.CompilerParams(
            vmem_limit_bytes=VMEM, collective_id=0, has_side_effects=True
        ),
        name="whole",
    )(sel, sel.reshape(1, SLOTS), k, v, q, g)


def body(query, keys, values, output_cotangent, select):
    row = lax.axis_index("y")
    flat = select.reshape(BLOCKS * CHOSEN_BLOCKS)
    row_select = lax.dynamic_slice_in_dim(flat, row * SLOTS, SLOTS, 0)
    dq, dk, dv = whole(row_select, keys, values, query, output_cotangent)
    rows = (Z * BLOCK_TOKENS, HEAD_SIZE)
    return dq, dk.reshape(rows), dv.reshape(rows)


def solution(mesh):
    groups = mesh.shape["grp"]
    grid = jax.sharding.Mesh(
        mesh.devices.reshape(-1, STRIPES, groups), ("y", "xc", "grp")
    )
    rows = ("y", "xc")
    in_specs = (P(rows + ("grp",), None),) * 4 + (P(None, "grp", None),)
    out_specs = (P(rows, "grp"),) * 3
    return jax.shard_map(
        body, mesh=grid, in_specs=in_specs, out_specs=out_specs, check_vma=False
    )
```

time: 251 us -> 180 us (0.72)
  waiting for transfers between devices: 63 us -> 0 us
  between operations: 14.1 us -> 0.67 us
  Pallas kernels: 165 us -> 173 us
  starting transfers between devices: 4.93 us -> 0 us
    reduce_scatter x1 -> x0, waiting for transfers between devices: 53.5 us -> none  [body(): row_sums = lax.psum_scatter(sums, 'y', scatter_dimension=0, tiled=True)]
    all_to_all x1 -> x0, waiting for transfers between devices: 9.48 us -> none  [body(): lax.all_to_all(row_sums, 'xc', split_axis=0, concat_axis=0, tiled=True)]
    pallas_call x2 -> x1, Pallas kernels: 165 us -> 173 us  [whole(): pl.pallas_call(whole_kernel, out_shape=(jax.ShapeDtypeStruct((Z * BLOCK_T...]
    all_to_all x1 -> x0, starting transfers between devices: 4.89 us -> none  [body(): lax.all_to_all(row_sums, 'xc', split_axis=0, concat_axis=0, tiled=True)]
    unnamed x4 -> x8, local copies, waits for them, and re-layouts: 1.81 us -> 4.89 us
  transfers between devices with their start and end apart: 2 -> 0, of which waited for: 2 -> 0; matrix products, arithmetic and copies ran while one was open for 0% -> 0% of each run, Pallas kernels for 0% -> 0%
where the time goes in v3:
time: 180 us
  Pallas kernels  173 us (96%)
  local copies, waits for them, and re-layouts  5.7 us (3%)
    pallas_call x1, Pallas kernels, whole(): pl.pallas_call(whole_kernel, out_shape=(jax.ShapeDtypeStruct((Z * BLOCK_T...  173 us
    unnamed x8, local copies, waits for them, and re-layouts  4.89 us

profile of v3, /device:TPU:1, one launch (start us, length us, event | category | flops | bytes accessed | tf_op | source)
XLA Modules:
  0.0 179.7 jit_solution(998988322353377426)
XLA Ops:
  0.6 0.8 copy.8
  1.5 0.1 reshape.18
  1.6 0.7 dynamic_slice.3.sel
  2.3 173.3 %whole.1 = (bf16[1024,512]{1,0:T(8,128)(2,1)}, bf16[8,128,128]{2,1,0:T(8,128)(2,1)}, bf16[8,128,128]{2,1,0:T(8,128)(2,1)}) custom-call(s32[512]{0:T(512)} %dynamic_slice.3.sel, s32[1,512]{1,0:T(1,128)} %bitcast.7, bf16[128,1024]{1,0:T(8,128)(2,1)} %k.1, bf16[128,1024]{1,0:T(8,128)(2,1)} %v.1, bf16[128,4096]{1,0:T(8,128)(2,1)} %q.1, bf16[128,4096]{1,0:T(8,128)(2,1)} %g.1), custom_call_target="tpu_custom_call" | custom-call | tf_op jit(solution)/shard_map/whole/pallas_call | solution.py:405
  175.6 0.0 copy-start.1
  175.6 2.3 %copy.12 = bf16[1024,512]{1,0:T(8,128)(2,1)} copy(bf16[1024,512]{1,0:T(8,128)(2,1)} %get-tuple-element.12) | data formatting | bytes 2097152
  177.9 0.0 copy-done.1
  177.9 0.0 copy-start
  177.9 0.7 copy.13
  178.6 0.3 copy-done
  179.0 0.7 copy.14
Async XLA Ops:
  175.6 2.3 %copy-start.1 = (bf16[8,128,128]{2,1,0:T(8,128)(2,1)S(1)}, bf16[8,128,128]{2,1,0:T(8,128)(2,1)}, u32[]{:S(2)}) copy-start(bf16[8,128,128]{2,1,0:T(8,128)(2,1)} %get-tuple-element.7) | copy-start | bytes 786436
  177.9 1.0 copy-start

commit v4 on v3

--- a/solution.py
+++ b/solution.py
@@ -36,7 +36,8 @@
 SLOTS = C * Z * CHOSEN_BLOCKS
 SHARE = C * Z
 BLOCKS = Y * SHARE
-HALF = SHARE // 2
+PARTS = 4
+PIECE = SHARE // PARTS
 STEPS = 4
 SPLITS = 4
 PER_SPLIT = Z // SPLITS
@@ -98,17 +99,17 @@
 
 def order_requests(sel_row, order):
     lane = lax.broadcasted_iota(jnp.int32, (1, SLOTS), 1)
-    key = jnp.where(lax.rem(lane, CHOSEN_BLOCKS) == 0, BLOCKS * SLOTS, sel_row * SLOTS + lane)
+    key = jnp.where(lane < SHARE, BLOCKS * SLOTS, sel_row * SLOTS + lane)
 
     def column(x):
         return jnp.broadcast_to(x, (128, SLOTS)).T[:, :1]
 
     index = lax.broadcasted_iota(jnp.int32, (SLOTS, 1), 0)
-    valid = lax.rem(index, CHOSEN_BLOCKS) != 0
+    valid = index >= SHARE
     chosen = column(sel_row)
     rank = jnp.sum((key < column(key)).astype(jnp.int32), axis=1, keepdims=True)
     rank = jnp.where(valid, rank, -2)
-    place = lax.div(index, CHOSEN_BLOCKS) * OTHERS + lax.rem(index, CHOSEN_BLOCKS) - 1
+    place = lax.rem(index, SHARE) * OTHERS + lax.div(index, SHARE) - 1
 
     def pick(mask, value):
         return jnp.sum(jnp.where(mask, value, 0), axis=0, keepdims=True)
@@ -124,11 +125,11 @@
 
 
 def whole_kernel(
-    sel, sel_row, k, v, q, g, dq, dk, dv,
+    sel, sel_rows, k, v, q, g, dq, dk, dv,
     kz, vz, qh, gh, tab_k, tab_v, out_k, out_v, in_k, in_v, dk_out, dv_out, ret_k, ret_v, probs, dscores,
-    dk_own, dv_own, runs, rs_out, rs_in, fin_out, fin_in, order_v, order,
+    dk_own, dv_own, k_runs, v_runs, rs_out, rs_in, fin_out, fin_in, order_v, order,
     z_send, z_recv, s_send, s_recv, ag_send, ag_recv, k_send, k_recv, v_send, v_recv,
-    rv_send, rv_recv, rk_send, rk_recv, rs_send, rs_recv, u_send, u_recv, own_sem,
+    rv_send, rv_recv, rk_send, rk_recv, rs_send, rs_recv, u_send, u_recv, own_sem, d_sem, l_send, l_recv,
 ):
     y, c, z = lax.axis_index("y"), lax.axis_index("xc"), lax.axis_index("grp")
 
@@ -142,67 +143,93 @@
         )
 
     barrier = pltpu.get_barrier_semaphore()
-    partners = [device(dz=d) for d in range(1, Z)] + [device(dc=d) for d in range(1, C)]
-    partners += [device(dy=1), device(dy=-1)]
+    partners = [device(dc=e, dz=d) for e in range(C) for d in range(Z) if e or d]
+    partners += [device(dy=way, dc=e) for way in (1, -1) for e in range(C)]
     for p in partners:
         pl.semaphore_signal(barrier, inc=1, device_id=p, device_id_type=pl.DeviceIdType.MESH)
     pl.semaphore_wait(barrier, len(partners))
 
-    by_head = ((k, HEAD_SIZE, kz), (v, HEAD_SIZE, vz), (q, WIDE, qh), (g, WIDE, gh))
+    by_head = (None, (v, HEAD_SIZE, vz), (q, WIDE, qh), (g, WIDE, gh))
 
     def z_copy(n, d):
         src, width, dst = by_head[n]
         to = lax.rem(z + d, Z)
         return remote(src.at[:, at(to, width)], dst.at[z], z_send.at[n, d], z_recv.at[n, d], device(dz=d))
 
-    for n in range(2):
+    def keys_copy(e, d):
+        to, head = lax.rem(c + e, C), lax.rem(z + d, Z)
+        return remote(
+            k.at[at(to, ROWS), at(head, HEAD_SIZE)], tab_k.at[y * SHARE + c * Z + z],
+            d_sem.at[0], d_sem.at[1], device(dc=e, dz=d),
+        )
+
+    def keys_all():
+        all_but_one = tab_k.at[pl.ds(0, SHARE - 1)]
+        return remote(all_but_one, all_but_one, d_sem.at[0], d_sem.at[1], device(dc=1))
+
+    for d in range(Z):
+        for e in range(C):
+            if d or e:
+                keys_copy(e, d).start()
+    for n in range(1, 4):
         for d in range(1, Z):
             z_copy(n, d).start()
-    for src, width, dst in by_head:
-        dst[z] = src[:, at(z, width)]
+    tab_k[y * SHARE + c * Z + z] = k[at(c, ROWS), at(z, HEAD_SIZE)]
+    vz[z] = v[:, at(z, HEAD_SIZE)]
+    own_q = pltpu.make_async_copy(q.at[:, at(z, WIDE)], qh.at[z], own_sem.at[3])
+    own_g = pltpu.make_async_copy(g.at[:, at(z, WIDE)], gh.at[z], own_sem.at[4])
+    own_q.start()
+    own_g.start()
 
     mine = at(y * C + c, Z)
-    to_table = ((kz, tab_k), (vz, tab_v))
 
     def s_copy(n, d):
-        src, tab = to_table[n]
         to = lax.rem(c + d, C)
-        return remote(src.at[:, at(to, ROWS)], tab.at[mine], s_send.at[n, d], s_recv.at[n, d], device(dc=d))
-
-    for n in range(2):
-        for d in range(1, Z):
-            z_copy(n, d).wait_recv()
-        for d in range(1, C):
-            s_copy(n, d).start()
-        src, tab = to_table[n]
-        tab[mine] = src[:, at(c, ROWS)]
-    for n in (2, 3):
-        for d in range(1, Z):
-            z_copy(n, d).start()
+        if n:
+            src, dst = vz.at[:, at(to, ROWS)], tab_v.at[mine]
+        else:
+            src, dst = tab_k.at[at(y * C + to, Z)], kz.at[:, at(c, ROWS)]
+        return remote(src, dst, s_send.at[n, d], s_recv.at[n, d], device(dc=d))
 
     def ring(n, s, way, half):
-        tab = to_table[n][1]
+        tab = (tab_k, tab_v)[n]
         owner = lax.rem(y - way * s + Y, Y)
-        part = tab.at[at(owner * 2 + half, HALF)]
+        part = tab.at[at(owner * PARTS + half, PIECE)]
         lane = 0 if way > 0 else 1
         return remote(part, part, ag_send.at[n, s, lane, half], ag_recv.at[n, s, lane, half], device(dy=way))
 
-    ring_order = ((1, 0), (-1, 1), (1, 1), (-1, 0))
+    ring_order = []
+    for n in range(PARTS):
+        ring_order += [(1, n), (-1, (n + PARTS // 2) % PARTS)]
 
     def ring_first(n):
         for way, half in ring_order:
             ring(n, 0, way, half).start()
 
     def ring_next(n, s):
-        for way, half in ring_order[: 2 if s == STEPS - 1 else 4]:
+        for way, half in ring_order[: PARTS if s == STEPS - 1 else 2 * PARTS]:
             ring(n, s - 1, way, half).wait_recv()
             ring(n, s, way, half).start()
 
     def ring_last(n):
-        for way, half in ring_order[2:]:
+        for way, half in ring_order[PARTS:]:
             ring(n, STEPS - 2, way, half).wait_recv()
-        for way, half in ring_order[:2]:
+        for way, half in ring_order[:PARTS]:
             ring(n, STEPS - 1, way, half).wait_recv()
+
+    def chosen_row():
+        two = sel_rows[:, at(lax.div(y, 2), 2 * SHARE)]
+        turned = pltpu.roll(two, SHARE, 1)
+        low = jnp.where(lax.rem(y, 2) == 0, two, turned)
+        high = jnp.where(lax.rem(y, 2) == 0, turned, two)
+        lane = lax.broadcasted_iota(jnp.int32, (1, 2 * SHARE), 1)
+        return jnp.concatenate(
+            [
+                jnp.where(lane < SHARE, low[j : j + 1], high[j + 1 : j + 2])
+                for j in range(0, CHOSEN_BLOCKS, 2)
+            ],
+            axis=1,
+        )
 
     def pack(tab, out, own, first, count):
         for d in range(C):
@@ -211,7 +238,7 @@
             @pl.loop(first, first + count)
             def _(i):
                 for j in range(OTHERS):
-                    rows = tab[sel[(to * Z + i) * CHOSEN_BLOCKS + 1 + j]]
+                    rows = tab[sel[1 + j, y * SHARE + to * Z + i]]
                     if d:
                         out[d, i * OTHERS + j] = rows
                     else:
@@ -237,13 +264,20 @@
         to = lax.rem(c + d, C)
         return remote(dk_out.at[to], ret_k.at[at(c, UNITS)], rk_send.at[d], rk_recv.at[d], device(dc=d))
 
-    for d in range(1, C):
-        s_copy(0, d).wait_recv()
+    keys_all().wait_recv()
     ring_first(0)
     for d in range(1, C):
-        s_copy(1, d).wait_recv()
+        s_copy(0, d).start()
+    kz[:, at(c, ROWS)] = tab_k[mine]
+    for d in range(1, Z):
+        z_copy(1, d).wait_recv()
+    for d in range(1, C):
+        s_copy(1, d).start()
+    tab_v[mine] = vz[:, at(c, ROWS)]
     for s in range(1, STEPS):
         ring_next(0, s)
+    for d in range(1, C):
+        s_copy(1, d).wait_recv()
     ring_first(1)
     ring_last(0)
     pack(tab_k, out_k, in_k, 0, Z)
@@ -251,7 +285,7 @@
         k_copy(d).start()
     for s in range(1, STEPS):
         ring_next(1, s)
-    order_requests(sel_row[...], order_v)
+    order_requests(chosen_row(), order_v)
     to_scalars = pltpu.make_async_copy(order_v, order, own_sem.at[2])
     to_scalars.start()
     to_scalars.wait()
@@ -262,10 +296,13 @@
         for d in range(1, C):
             v_copy(d, n).start()
 
+    own_q.wait()
+    own_g.wait()
     for n in (2, 3):
         for d in range(1, Z):
             z_copy(n, d).wait_recv()
     for d in range(1, C):
+        s_copy(0, d).wait_recv()
         k_copy(d).wait_recv()
 
     @pl.loop(0, SPLITS)
@@ -276,9 +313,9 @@
         @pl.loop(0, PER_SPLIT)
         def _(m):
             i = n * PER_SPLIT + m
-            first = (c * Z + i) * CHOSEN_BLOCKS
+            block = y * SHARE + c * Z + i
             attention_block(
-                i, sel[first], lambda j: sel[first + j],
+                i, block, lambda j: sel[j, block],
                 qh, gh, kz, vz, in_k, in_v, dq, dk_own, dv_own, dk_out, dv_out, probs, dscores,
             )
 
@@ -295,9 +332,11 @@
     own_k.wait()
 
     nothing = jnp.zeros((ROWS, HEAD_SIZE), jnp.float32)
-    runs[REQUESTS] = nothing
-
-    def run_sums(ret):
+    all_runs = (k_runs, v_runs)
+
+    def run_sums(ret, runs):
+        runs[REQUESTS] = nothing
+
         def add(p, total):
             total = ret[order[0, p]].astype(jnp.float32) + jnp.where(order[1, p] == 1, total, 0.0)
             runs[p] = total
@@ -318,63 +357,85 @@
         if arrived:
             rs_copy(n, s - 1, way, half).wait_recv()
 
-        @pl.loop(0, HALF, unroll=8)
+        @pl.loop(0, PIECE, unroll=8)
         def _(t):
-            total = runs[order[2, owner * SHARE + half * HALF + t]]
+            total = all_runs[n][order[2, owner * SHARE + half * PIECE + t]]
             if arrived:
                 total += rs_in[n, lane, s - 1, half, t].astype(jnp.float32)
             rs_out[n, lane, s, half, t] = total.astype(jnp.bfloat16)
 
-        rs_copy(n, s, way, half).start()
+        if s < STEPS - 1:
+            rs_copy(n, s, way, half).start()
+        else:
+            for m in range(C // PARTS):
+                last_copy(n, way, half, m).start()
+
+    def last_copy(n, way, half, m):
+        lane = 0 if way > 0 else 1
+        to = half * (C // PARTS) + m
+        e = lax.rem(to - c + C, C)
+        return remote(
+            rs_out.at[n, lane, STEPS - 1, half, pl.ds(m * Z, Z)], fin_in.at[n, lane, :, at(c, ROWS)],
+            l_send.at[n, lane, e], l_recv.at[n, lane, e], (lax.rem(y + way + Y, Y), to, z),
+        )
 
     def u_copy(n, d):
         to = lax.rem(c + d, C)
         return remote(
-            fin_out.at[n, at(to, Z)], fin_in.at[n, :, at(c, ROWS)], u_send.at[n, d], u_recv.at[n, d], device(dc=d)
-        )
-
-    def reduce(n):
-        for way, half in ring_order[:2]:
+            fin_out.at[n, at(to, Z)], fin_in.at[n, 2, :, at(c, ROWS)], u_send.at[n, d], u_recv.at[n, d], device(dc=d)
+        )
+
+    def reduce_own(n):
+        @pl.loop(0, SHARE, unroll=8)
+        def _(t):
+            fin_out[n, t] = all_runs[n][order[2, y * SHARE + t]].astype(jnp.bfloat16)
+
+        for d in range(1, C):
+            u_copy(n, d).start()
+        fin_in[n, 2, :, at(c, ROWS)] = fin_out[n, at(c, Z)]
+
+    def reduce_first(n):
+        for way, half in ring_order[:PARTS]:
             rs_step(n, 0, way, half, False)
-        for way, half in ring_order[2:]:
+        for way, half in ring_order[PARTS:]:
             rs_step(n, 1, way, half, False)
-        for way, half in ring_order[:2]:
+
+    def reduce_next(n):
+        for way, half in ring_order[:PARTS]:
             rs_step(n, 1, way, half, True)
         for s in range(2, STEPS):
-            for way, half in ring_order[2:] + ring_order[:2]:
+            for way, half in ring_order[PARTS:] + ring_order[:PARTS]:
                 rs_step(n, s, way, half, True)
-        for half in (1, 0):
-            for way in (1, -1):
-                rs_copy(n, STEPS - 1, way, half).wait_recv()
-
-            @pl.loop(0, HALF, unroll=8)
-            def _(t):
-                total = runs[order[2, y * SHARE + half * HALF + t]]
-                for lane in range(2):
-                    total += rs_in[n, lane, STEPS - 1, half, t].astype(jnp.float32)
-                fin_out[n, half * HALF + t] = total.astype(jnp.bfloat16)
-
-        for d in range(1, C):
-            u_copy(n, d).start()
-        fin_in[n, :, at(c, ROWS)] = fin_out[n, at(c, Z)]
 
     for n in range(SPLITS):
         for d in range(1, C):
             rv_copy(d, n).wait_recv()
-    run_sums(ret_v)
-    reduce(1)
+    run_sums(ret_v, v_runs)
+    reduce_first(1)
+    reduce_own(1)
+    reduce_next(1)
     for d in range(1, C):
         rk_copy(d).wait_recv()
-    run_sums(ret_k)
-    reduce(0)
+    run_sums(ret_k, k_runs)
+    reduce_first(0)
+    reduce_own(0)
+    reduce_next(0)
     for n, own, out in ((1, dv_own, dv), (0, dk_own, dk)):
         for d in range(1, C):
             u_copy(n, d).wait_recv()
+        for way in (1, -1):
+            for half in range(PARTS):
+                for m in range(C // PARTS):
+                    last_copy(n, way, half, m).wait_recv()
         for i in range(Z):
-            out[i] = (fin_in[n, i].astype(jnp.float32) + own[i]).astype(jnp.bfloat16)
-
+            total = own[i]
+            for lane in range(3):
+                total += fin_in[n, lane, i].astype(jnp.float32)
+            out[i] = total.astype(jnp.bfloat16)
+
+    keys_all().wait_send()
     for d in range(1, Z):
-        for n in range(4):
+        for n in range(1, 4):
             z_copy(n, d).wait_send()
     for d in range(1, C):
         for n in range(2):
@@ -387,10 +448,14 @@
             rv_copy(d, n).wait_send()
     for n in range(2):
         for s in range(STEPS):
-            for way, half in ring_order[: 2 if s == STEPS - 1 else 4]:
+            for way, half in ring_order[: PARTS if s == STEPS - 1 else 2 * PARTS]:
                 ring(n, s, way, half).wait_send()
-            for way, half in ring_order[: 2 if s == 0 else 4]:
-                rs_copy(n, s, way, half).wait_send()
+            for way, half in ring_order[: PARTS if s == 0 else 2 * PARTS]:
+                if s < STEPS - 1:
+                    rs_copy(n, s, way, half).wait_send()
+                else:
+                    for m in range(C // PARTS):
+                        last_copy(n, way, half, m).wait_send()
 
 
 def whole(sel, k, v, q, g):
@@ -401,7 +466,7 @@
     units = (C, UNITS, ROWS, HEAD_SIZE)
     table = (BLOCKS, ROWS, HEAD_SIZE)
     heads = (Z, BLOCK_TOKENS, HEAD_SIZE)
-    steps = (2, 2, STEPS, 2, HALF, ROWS, HEAD_SIZE)
+    steps = (2, 2, STEPS, PARTS, PIECE, ROWS, HEAD_SIZE)
     return pl.pallas_call(
         whole_kernel,
         out_shape=(
@@ -409,7 +474,7 @@
             jax.ShapeDtypeStruct(heads, jnp.bfloat16),
             jax.ShapeDtypeStruct(heads, jnp.bfloat16),
         ),
-        in_specs=[pl.BlockSpec(memory_space=pltpu.SMEM)] + [vmem] * 5,
+        in_specs=[pl.BlockSpec(memory_space=pltpu.SMEM)] + [vmem] * 3 + [pl.BlockSpec(memory_space=pl.ANY)] * 2,
         out_specs=[vmem] * 3,
         scratch_shapes=[bf16(*heads)] * 2
         + [bf16(Z, BLOCK_TOKENS, WIDE)] * 2
@@ -418,33 +483,51 @@
         + [bf16(REQUESTS, ROWS, HEAD_SIZE)] * 2
         + [bf16(KEYS, WIDE)] * 2
         + [f32(*heads)] * 2
-        + [f32(REQUESTS + 8, ROWS, HEAD_SIZE)]
+        + [f32(REQUESTS + 8, ROWS, HEAD_SIZE)] * 2
         + [bf16(*steps)] * 2
         + [bf16(2, SHARE, ROWS, HEAD_SIZE)]
-        + [bf16(2, *heads)]
+        + [bf16(2, 3, *heads)]
         + [pltpu.VMEM((8, SLOTS), jnp.int32), pltpu.SMEM((8, SLOTS), jnp.int32)]
         + [dma(4, Z)] * 2
         + [dma(2, C)] * 2
-        + [dma(2, STEPS, 2, 2)] * 2
+        + [dma(2, STEPS, 2, PARTS)] * 2
         + [dma(C)] * 2
         + [dma(C, SPLITS)] * 2
         + [dma(C, SPLITS)] * 2
         + [dma(C)] * 2
-        + [dma(2, 2, STEPS, 2)] * 2
+        + [dma(2, 2, STEPS, PARTS)] * 2
         + [dma(2, C)] * 2
-        + [dma(3)],
+        + [dma(5)]
+        + [dma(2)]
+        + [dma(2, 2, C)] * 2,
         compiler_params=pltpu.CompilerParams(
             vmem_limit_bytes=VMEM, collective_id=0, has_side_effects=True
         ),
         name="whole",
-    )(sel, sel.reshape(1, SLOTS), k, v, q, g)
+    )(sel, sel, k, v, q, g)
+
+
+def finish_kernel(dq, dk, dv, dq_out, dk_out, dv_out):
+    dq_out[...] = dq[...]
+    dk_out[...] = dk[...]
+    dv_out[...] = dv[...]
+
+
+def finish(*arrays):
+    vmem = pl.BlockSpec(memory_space=pltpu.VMEM)
+    return pl.pallas_call(
+        finish_kernel,
+        out_shape=tuple(jax.ShapeDtypeStruct(a.shape, a.dtype) for a in arrays),
+        in_specs=[vmem] * len(arrays),
+        out_specs=[vmem] * len(arrays),
+        compiler_params=pltpu.CompilerParams(vmem_limit_bytes=VMEM),
+        name="finish",
+    )(*arrays)
 
 
 def body(query, keys, values, output_cotangent, select):
-    row = lax.axis_index("y")
-    flat = select.reshape(BLOCKS * CHOSEN_BLOCKS)
-    row_select = lax.dynamic_slice_in_dim(flat, row * SLOTS, SLOTS, 0)
-    dq, dk, dv = whole(row_select, keys, values, query, output_cotangent)
+    by_slot = select.reshape(BLOCKS, CHOSEN_BLOCKS).T
+    dq, dk, dv = finish(*whole(by_slot, keys, values, query, output_cotangent))
     rows = (Z * BLOCK_TOKENS, HEAD_SIZE)
     return dq, dk.reshape(rows), dv.reshape(rows)
 

time: 180 us -> 167 us (0.928)
  Pallas kernels: 173 us -> 166 us
  local copies, waits for them, and re-layouts: 5.7 us -> 0 us
    pallas_call x1, Pallas kernels: 173 us -> 164 us  [whole(): pl.pallas_call(whole_kernel, out_shape=(jax.ShapeDtypeStruct((Z * BLOCK_T...]
    unnamed x8 -> x0, local copies, waits for them, and re-layouts: 4.89 us -> none
    pallas_call x0 -> x1, Pallas kernels: none -> 2.5 us  [finish(): pl.pallas_call(finish_kernel, out_shape=tuple((jax.ShapeDtypeStruct(a.sha...]
where the time goes in v4:
time: 167 us
  Pallas kernels  166 us (99%)
    pallas_call x1, Pallas kernels, whole(): pl.pallas_call(whole_kernel, out_shape=(jax.ShapeDtypeStruct((Z * BLOCK_T...  164 us

profile of v4, /device:TPU:1, one launch (start us, length us, event | category | flops | bytes accessed | tf_op | source)
XLA Modules:
  0.0 167.1 jit_solution(13046480423589742608)
XLA Ops:
  0.6 164.0 %whole.1 = (bf16[1024,512]{1,0:T(8,128)(2,1)}, bf16[8,128,128]{2,1,0:T(8,128)(2,1)}, bf16[8,128,128]{2,1,0:T(8,128)(2,1)}) custom-call(s32[8,512]{1,0:T(8,128)} %bitcast.5, s32[8,512]{1,0:T(8,128)} %bitcast.6, bf16[128,1024]{1,0:T(8,128)(2,1)} %k.1, bf16[128,1024]{1,0:T(8,128)(2,1)} %v.1, bf16[128,4096]{1,0:T(8,128)(2,1)} %q.1, bf16[128,4096]{1,0:T(8,128)(2,1)} %g.1), custom_call_target="tpu_custom_call" | custom-call | tf_op jit(solution)/shard_map/whole/pallas_call | solution.py:470
  164.6 2.5 %finish.1 = (bf16[1024,512]{1,0:T(8,128)(2,1)}, bf16[8,128,128]{2,1,0:T(8,128)(2,1)}, bf16[8,128,128]{2,1,0:T(8,128)(2,1)}) custom-call(bf16[1024,512]{1,0:T(8,128)(2,1)} %get-tuple-element.9.dq, bf16[8,128,128]{2,1,0:T(8,128)(2,1)} %get-tuple-element.10.dk, bf16[8,128,128]{2,1,0:T(8,128)(2,1)} %get-tuple-element.11.dv), custom_call_target="tpu_custom_call" | custom-call | tf_op jit(solution)/shard_map/finish/pallas_call | solution.py:518

commit v5 on v4

--- a/solution.py
+++ b/solution.py
@@ -39,21 +39,20 @@
 PARTS = 4
 PIECE = SHARE // PARTS
 STEPS = 4
+TURN_STEP = 2
 SPLITS = 4
 PER_SPLIT = Z // SPLITS
 WIDE = GROUP * HEAD_SIZE
+OTHERS_SHAPE = (STRIPES, OTHERS, ROWS, HEAD_SIZE)
 
 
 def at(index, size):
     return pl.ds(pl.multiple_of(index * size, size), size)
 
 
-def attention_block(
-    i, own, sel_at, q_ref, g_ref, kz, vz, k_ref, v_ref, dq_ref, dk_own, dv_own, dk_ref, dv_ref, probs, dscores
-):
+def probs_block(i, own, sel_at, q_ref, g_ref, kz, k_ref, dv_own, dv_ref, probs):
     units = pl.ds(i * OTHERS, OTHERS)
     keys = jnp.concatenate([kz[i], k_ref[:, units].reshape(OTHER_KEYS, HEAD_SIZE)], 0)
-    vals = jnp.concatenate([vz[i], v_ref[:, units].reshape(OTHER_KEYS, HEAD_SIZE)], 0)
     row = lax.broadcasted_iota(jnp.int32, (BLOCK_TOKENS, BLOCK_TOKENS), 0)
     token = lax.broadcasted_iota(jnp.int32, (BLOCK_TOKENS, BLOCK_TOKENS), 1)
     own_bias = jnp.where(row <= token, 0.0, -jnp.inf).astype(jnp.float32)
@@ -67,28 +66,35 @@
         axis=1,
     ).reshape(OTHER_KEYS, BLOCK_TOKENS)
     bias = jnp.concatenate([own_bias, other_bias], 0)
-    q_parts, g_parts = [], []
     for h in range(GROUP):
         cols = pl.ds(h * HEAD_SIZE, HEAD_SIZE)
-        q, g = q_ref[i, :, cols], g_ref[i, :, cols]
-        q_parts.append(q)
-        g_parts.append(g)
-        scores = nt(keys, q) * FACTOR + bias
+        scores = nt(keys, q_ref[i, :, cols]) * FACTOR + bias
         highest = jnp.max(scores, axis=0, keepdims=True)
         weights = jnp.exp(scores - highest)
         prob = weights * (1.0 / jnp.sum(weights, axis=0, keepdims=True))
-        low = prob.astype(jnp.bfloat16)
-        dprobs = nt(vals, g)
-        delta = jnp.sum(low.astype(jnp.float32) * dprobs, axis=0, keepdims=True)
-        probs[:, cols] = low
+        probs[i, :, cols] = prob.astype(jnp.bfloat16)
+    dv = nn(probs[i], by_head_rows(g_ref, i))
+    dv_own[i] = dv[:BLOCK_TOKENS]
+    dv_ref[:, units] = dv[BLOCK_TOKENS:].astype(jnp.bfloat16).reshape(OTHERS_SHAPE)
+
+
+def by_head_rows(ref, i):
+    return jnp.concatenate([ref[i, :, h * HEAD_SIZE : (h + 1) * HEAD_SIZE] for h in range(GROUP)], 0)
+
+
+def scores_block(i, q_ref, g_ref, kz, vz, k_ref, v_ref, dq_ref, dk_own, dk_ref, probs, dscores):
+    units = pl.ds(i * OTHERS, OTHERS)
+    keys = jnp.concatenate([kz[i], k_ref[:, units].reshape(OTHER_KEYS, HEAD_SIZE)], 0)
+    vals = jnp.concatenate([vz[i], v_ref[:, units].reshape(OTHER_KEYS, HEAD_SIZE)], 0)
+    for h in range(GROUP):
+        cols = pl.ds(h * HEAD_SIZE, HEAD_SIZE)
+        prob = probs[i, :, cols].astype(jnp.float32)
+        dprobs = nt(vals, g_ref[i, :, cols])
+        delta = jnp.sum(prob * dprobs, axis=0, keepdims=True)
         dscores[:, cols] = (prob * (dprobs - delta)).astype(jnp.bfloat16)
-    others = (STRIPES, OTHERS, ROWS, HEAD_SIZE)
-    dv = nn(probs[...], jnp.concatenate(g_parts, 0))
-    dv_own[i] = dv[:BLOCK_TOKENS]
-    dv_ref[:, units] = dv[BLOCK_TOKENS:].astype(jnp.bfloat16).reshape(others)
-    dk = nn(dscores[...], jnp.concatenate(q_parts, 0)) * FACTOR
+    dk = nn(dscores[...], by_head_rows(q_ref, i)) * FACTOR
     dk_own[i] = dk[:BLOCK_TOKENS]
-    dk_ref[:, units] = dk[BLOCK_TOKENS:].astype(jnp.bfloat16).reshape(others)
+    dk_ref[:, units] = dk[BLOCK_TOKENS:].astype(jnp.bfloat16).reshape(OTHERS_SHAPE)
     dq_t = nn(keys.T, dscores[...]) * FACTOR
     for h in range(GROUP):
         cols = pl.ds(h * HEAD_SIZE, HEAD_SIZE)
@@ -127,9 +133,9 @@
 def whole_kernel(
     sel, sel_rows, k, v, q, g, dq, dk, dv,
     kz, vz, qh, gh, tab_k, tab_v, out_k, out_v, in_k, in_v, dk_out, dv_out, ret_k, ret_v, probs, dscores,
-    dk_own, dv_own, k_runs, v_runs, rs_out, rs_in, fin_out, fin_in, order_v, order,
+    dk_own, dv_own, runs, rs_out, rs_in, fin_out, fin_in, order_v, order,
     z_send, z_recv, s_send, s_recv, ag_send, ag_recv, k_send, k_recv, v_send, v_recv,
-    rv_send, rv_recv, rk_send, rk_recv, rs_send, rs_recv, u_send, u_recv, own_sem, d_sem, l_send, l_recv,
+    rv_send, rv_recv, rk_send, rk_recv, rs_send, rs_recv, u_send, u_recv, own_sem, d_sem, l_send, l_recv, turn,
 ):
     y, c, z = lax.axis_index("y"), lax.axis_index("xc"), lax.axis_index("grp")
 
@@ -141,6 +147,9 @@
             src_ref=src, dst_ref=dst, send_sem=send, recv_sem=recv,
             device_id=target, device_id_type=pl.DeviceIdType.MESH,
         )
+
+    tab_k[...] = jnp.zeros_like(tab_k)
+    tab_v[...] = jnp.zeros_like(tab_v)
 
     barrier = pltpu.get_barrier_semaphore()
     partners = [device(dc=e, dz=d) for e in range(C) for d in range(Z) if e or d]
@@ -150,6 +159,12 @@
     pl.semaphore_wait(barrier, len(partners))
 
     by_head = (None, (v, HEAD_SIZE, vz), (q, WIDE, qh), (g, WIDE, gh))
+
+    core = lax.rem(c, 2)
+    sibling = device(dc=C + 1 - 2 * core)
+
+    def next_turn(n):
+        pl.semaphore_signal(turn.at[n], inc=1, device_id=sibling, device_id_type=pl.DeviceIdType.MESH)
 
     def z_copy(n, d):
         src, width, dst = by_head[n]
@@ -202,20 +217,35 @@
     for n in range(PARTS):
         ring_order += [(1, n), (-1, (n + PARTS // 2) % PARTS)]
 
+    def hops(way, half):
+        return STEPS if (way, half) in ring_order[:PARTS] else STEPS - 1
+
+    def ring_sent(s, way, half):
+        return y != Y - 1 if way > 0 else lax.rem(y + s, Y) < hops(way, half)
+
+    def ring_received(s, way, half):
+        return y != 0 if way > 0 else lax.rem(y + s + 1, Y) < hops(way, half)
+
+    def ring_start(n, s, way, half):
+        pl.when(ring_sent(s, way, half))(lambda: ring(n, s, way, half).start())
+
+    def ring_wait(n, s, way, half):
+        pl.when(ring_received(s, way, half))(lambda: ring(n, s, way, half).wait_recv())
+
     def ring_first(n):
         for way, half in ring_order:
-            ring(n, 0, way, half).start()
+            ring_start(n, 0, way, half)
 
     def ring_next(n, s):
         for way, half in ring_order[: PARTS if s == STEPS - 1 else 2 * PARTS]:
-            ring(n, s - 1, way, half).wait_recv()
-            ring(n, s, way, half).start()
+            ring_wait(n, s - 1, way, half)
+            ring_start(n, s, way, half)
 
     def ring_last(n):
         for way, half in ring_order[PARTS:]:
-            ring(n, STEPS - 2, way, half).wait_recv()
+            ring_wait(n, STEPS - 2, way, half)
         for way, half in ring_order[:PARTS]:
-            ring(n, STEPS - 1, way, half).wait_recv()
+            ring_wait(n, STEPS - 1, way, half)
 
     def chosen_row():
         two = sel_rows[:, at(lax.div(y, 2), 2 * SHARE)]
@@ -265,7 +295,12 @@
         return remote(dk_out.at[to], ret_k.at[at(c, UNITS)], rk_send.at[d], rk_recv.at[d], device(dc=d))
 
     keys_all().wait_recv()
-    ring_first(0)
+
+    @pl.when(core == 0)
+    def _():
+        ring_first(0)
+        ring_next(0, 1)
+
     for d in range(1, C):
         s_copy(0, d).start()
     kz[:, at(c, ROWS)] = tab_k[mine]
@@ -274,17 +309,33 @@
     for d in range(1, C):
         s_copy(1, d).start()
     tab_v[mine] = vz[:, at(c, ROWS)]
-    for s in range(1, STEPS):
+
+    @pl.when(core == 1)
+    def _():
+        pl.semaphore_wait(turn.at[0], 1)
+        ring_first(0)
+        ring_next(0, 1)
+
+    for s in range(2, STEPS):
         ring_next(0, s)
+        if s == TURN_STEP:
+            next_turn(core)
     for d in range(1, C):
         s_copy(1, d).wait_recv()
-    ring_first(1)
     ring_last(0)
     pack(tab_k, out_k, in_k, 0, Z)
     for d in range(1, C):
         k_copy(d).start()
+    pl.semaphore_wait(turn.at[1 + core], 1)
+    ring_first(1)
     for s in range(1, STEPS):
         ring_next(1, s)
+        if s == TURN_STEP:
+
+            @pl.when(core == 0)
+            def _():
+                next_turn(2)
+
     order_requests(chosen_row(), order_v)
     to_scalars = pltpu.make_async_copy(order_v, order, own_sem.at[2])
     to_scalars.start()
@@ -307,23 +358,25 @@
 
     @pl.loop(0, SPLITS)
     def _(n):
-        for d in range(1, C):
-            v_copy(d, n).wait_recv()
-
         @pl.loop(0, PER_SPLIT)
         def _(m):
             i = n * PER_SPLIT + m
             block = y * SHARE + c * Z + i
-            attention_block(
-                i, block, lambda j: sel[j, block],
-                qh, gh, kz, vz, in_k, in_v, dq, dk_own, dv_own, dk_out, dv_out, probs, dscores,
-            )
+            probs_block(i, block, lambda j: sel[j, block], qh, gh, kz, in_k, dv_own, dv_out, probs)
 
         for d in range(1, C):
             rv_copy(d, n).start()
 
-    for d in range(1, C):
-        rk_copy(d).start()
+    @pl.loop(0, SPLITS)
+    def _(n):
+        for d in range(1, C):
+            v_copy(d, n).wait_recv()
+
+        @pl.loop(0, PER_SPLIT)
+        def _(m):
+            i = n * PER_SPLIT + m
+            scores_block(i, qh, gh, kz, vz, in_k, in_v, dq, dk_own, dk_out, probs, dscores)
+
     own_v = pltpu.make_async_copy(dv_out.at[c], ret_v.at[at(c, UNITS)], own_sem.at[0])
     own_k = pltpu.make_async_copy(dk_out.at[c], ret_k.at[at(c, UNITS)], own_sem.at[1])
     own_v.start()
@@ -332,11 +385,9 @@
     own_k.wait()
 
     nothing = jnp.zeros((ROWS, HEAD_SIZE), jnp.float32)
-    all_runs = (k_runs, v_runs)
-
-    def run_sums(ret, runs):
-        runs[REQUESTS] = nothing
-
+    runs[REQUESTS] = nothing
+
+    def run_sums(ret):
         def add(p, total):
             total = ret[order[0, p]].astype(jnp.float32) + jnp.where(order[1, p] == 1, total, 0.0)
             runs[p] = total
@@ -351,24 +402,35 @@
             rs_send.at[n, lane, s, half], rs_recv.at[n, lane, s, half], device(dy=way),
         )
 
+    def rs_sent(s, way, half):
+        if way > 0:
+            return lax.rem(y + STEPS - s, Y) < hops(way, half)
+        return y >= STEPS - s
+
     def rs_step(n, s, way, half, arrived):
         lane = 0 if way > 0 else 1
         owner = lax.rem(y + way * (STEPS - s) + Y, Y)
-        if arrived:
-            rs_copy(n, s - 1, way, half).wait_recv()
-
-        @pl.loop(0, PIECE, unroll=8)
-        def _(t):
-            total = all_runs[n][order[2, owner * SHARE + half * PIECE + t]]
-            if arrived:
-                total += rs_in[n, lane, s - 1, half, t].astype(jnp.float32)
-            rs_out[n, lane, s, half, t] = total.astype(jnp.bfloat16)
-
-        if s < STEPS - 1:
-            rs_copy(n, s, way, half).start()
-        else:
-            for m in range(C // PARTS):
-                last_copy(n, way, half, m).start()
+
+        @pl.when(rs_sent(s, way, half))
+        def _():
+            if arrived and way > 0:
+                rs_copy(n, s - 1, way, half).wait_recv()
+            elif arrived:
+                pl.when(y != Y - 1)(lambda: rs_copy(n, s - 1, way, half).wait_recv())
+
+            @pl.loop(0, PIECE, unroll=8)
+            def _(t):
+                total = runs[order[2, owner * SHARE + half * PIECE + t]]
+                if arrived:
+                    before = rs_in[n, lane, s - 1, half, t].astype(jnp.float32)
+                    total += before if way > 0 else jnp.where(y != Y - 1, before, 0.0)
+                rs_out[n, lane, s, half, t] = total.astype(jnp.bfloat16)
+
+            if s < STEPS - 1:
+                rs_copy(n, s, way, half).start()
+            else:
+                for m in range(C // PARTS):
+                    last_copy(n, way, half, m).start()
 
     def last_copy(n, way, half, m):
         lane = 0 if way > 0 else 1
@@ -388,7 +450,7 @@
     def reduce_own(n):
         @pl.loop(0, SHARE, unroll=8)
         def _(t):
-            fin_out[n, t] = all_runs[n][order[2, y * SHARE + t]].astype(jnp.bfloat16)
+            fin_out[n, t] = runs[order[2, y * SHARE + t]].astype(jnp.bfloat16)
 
         for d in range(1, C):
             u_copy(n, d).start()
@@ -410,27 +472,35 @@
     for n in range(SPLITS):
         for d in range(1, C):
             rv_copy(d, n).wait_recv()
-    run_sums(ret_v, v_runs)
+    for d in range(1, C):
+        rk_copy(d).start()
+    run_sums(ret_v)
     reduce_first(1)
     reduce_own(1)
     reduce_next(1)
     for d in range(1, C):
         rk_copy(d).wait_recv()
-    run_sums(ret_k, k_runs)
+    run_sums(ret_k)
     reduce_first(0)
     reduce_own(0)
     reduce_next(0)
+    from_below = y < jnp.where(c < C // 2, hops(1, 0), hops(1, PARTS - 1))
+    from_above = y != Y - 1
     for n, own, out in ((1, dv_own, dv), (0, dk_own, dk)):
         for d in range(1, C):
             u_copy(n, d).wait_recv()
-        for way in (1, -1):
-            for half in range(PARTS):
-                for m in range(C // PARTS):
-                    last_copy(n, way, half, m).wait_recv()
+        for way, received in ((1, from_below), (-1, from_above)):
+
+            @pl.when(received)
+            def _():
+                for half in range(PARTS):
+                    for m in range(C // PARTS):
+                        last_copy(n, way, half, m).wait_recv()
+
         for i in range(Z):
-            total = own[i]
-            for lane in range(3):
-                total += fin_in[n, lane, i].astype(jnp.float32)
+            total = own[i] + fin_in[n, 2, i].astype(jnp.float32)
+            total += jnp.where(from_below, fin_in[n, 0, i].astype(jnp.float32), 0.0)
+            total += jnp.where(from_above, fin_in[n, 1, i].astype(jnp.float32), 0.0)
             out[i] = total.astype(jnp.bfloat16)
 
     keys_all().wait_send()
@@ -449,13 +519,16 @@
     for n in range(2):
         for s in range(STEPS):
             for way, half in ring_order[: PARTS if s == STEPS - 1 else 2 * PARTS]:
-                ring(n, s, way, half).wait_send()
+                pl.when(ring_sent(s, way, half))(lambda: ring(n, s, way, half).wait_send())
             for way, half in ring_order[: PARTS if s == 0 else 2 * PARTS]:
-                if s < STEPS - 1:
-                    rs_copy(n, s, way, half).wait_send()
-                else:
-                    for m in range(C // PARTS):
-                        last_copy(n, way, half, m).wait_send()
+
+                @pl.when(rs_sent(s, way, half))
+                def _():
+                    if s < STEPS - 1:
+                        rs_copy(n, s, way, half).wait_send()
+                    else:
+                        for m in range(C // PARTS):
+                            last_copy(n, way, half, m).wait_send()
 
 
 def whole(sel, k, v, q, g):
@@ -481,9 +554,9 @@
         + [bf16(*table)] * 2
         + [bf16(*units)] * 6
         + [bf16(REQUESTS, ROWS, HEAD_SIZE)] * 2
-        + [bf16(KEYS, WIDE)] * 2
+        + [bf16(Z, KEYS, WIDE), bf16(KEYS, WIDE)]
         + [f32(*heads)] * 2
-        + [f32(REQUESTS + 8, ROWS, HEAD_SIZE)] * 2
+        + [f32(REQUESTS + 8, ROWS, HEAD_SIZE)]
         + [bf16(*steps)] * 2
         + [bf16(2, SHARE, ROWS, HEAD_SIZE)]
         + [bf16(2, 3, *heads)]
@@ -492,14 +565,14 @@
         + [dma(2, C)] * 2
         + [dma(2, STEPS, 2, PARTS)] * 2
         + [dma(C)] * 2
-        + [dma(C, SPLITS)] * 2
-        + [dma(C, SPLITS)] * 2
+        + [dma(C, SPLITS)] * 4
         + [dma(C)] * 2
         + [dma(2, 2, STEPS, PARTS)] * 2
         + [dma(2, C)] * 2
         + [dma(5)]
         + [dma(2)]
-        + [dma(2, 2, C)] * 2,
+        + [dma(2, 2, C)] * 2
+        + [pltpu.SemaphoreType.REGULAR((3,))],
         compiler_params=pltpu.CompilerParams(
             vmem_limit_bytes=VMEM, collective_id=0, has_side_effects=True
         ),

time: 167 us -> 163 us (0.976); the launches traced: 167 us -> 161 us
  Pallas kernels: 166 us -> 161 us
    pallas_call x1, Pallas kernels: 164 us -> 158 us  [whole(): pl.pallas_call(whole_kernel, out_shape=(jax.ShapeDtypeStruct((Z * BLOCK_T...]
where the time goes in v5:
time: 163 us; the launch traced here: 161 us
  Pallas kernels  161 us (99%)
    pallas_call x1, Pallas kernels, whole(): pl.pallas_call(whole_kernel, out_shape=(jax.ShapeDtypeStruct((Z * BLOCK_T...  158 us

profile of v5, /device:TPU:1, one launch (start us, length us, event | category | flops | bytes accessed | tf_op | source)
XLA Modules:
  0.0 161.4 jit_solution(7792407533232008324)
XLA Ops:
  0.6 158.2 %whole.1 = (bf16[1024,512]{1,0:T(8,128)(2,1)}, bf16[8,128,128]{2,1,0:T(8,128)(2,1)}, bf16[8,128,128]{2,1,0:T(8,128)(2,1)}) custom-call(s32[8,512]{1,0:T(8,128)} %bitcast.5, s32[8,512]{1,0:T(8,128)} %bitcast.6, bf16[128,1024]{1,0:T(8,128)(2,1)} %k.1, bf16[128,1024]{1,0:T(8,128)(2,1)} %v.1, bf16[128,4096]{1,0:T(8,128)(2,1)} %q.1, bf16[128,4096]{1,0:T(8,128)(2,1)} %g.1), custom_call_target="tpu_custom_call" | custom-call | tf_op jit(solution)/shard_map/whole/pallas_call | solution.py:543
  158.9 2.5 %finish.1 = (bf16[1024,512]{1,0:T(8,128)(2,1)}, bf16[8,128,128]{2,1,0:T(8,128)(2,1)}, bf16[8,128,128]{2,1,0:T(8,128)(2,1)}) custom-call(bf16[1024,512]{1,0:T(8,128)(2,1)} %get-tuple-element.9.dq, bf16[8,128,128]{2,1,0:T(8,128)(2,1)} %get-tuple-element.10.dk, bf16[8,128,128]{2,1,0:T(8,128)(2,1)} %get-tuple-element.11.dv), custom_call_target="tpu_custom_call" | custom-call | tf_op jit(solution)/shard_map/finish/pallas_call | solution.py:591

commit v6 on v5

--- a/solution.py
+++ b/solution.py
@@ -148,9 +148,6 @@
             device_id=target, device_id_type=pl.DeviceIdType.MESH,
         )
 
-    tab_k[...] = jnp.zeros_like(tab_k)
-    tab_v[...] = jnp.zeros_like(tab_v)
-
     barrier = pltpu.get_barrier_semaphore()
     partners = [device(dc=e, dz=d) for e in range(C) for d in range(Z) if e or d]
     partners += [device(dy=way, dc=e) for way in (1, -1) for e in range(C)]
@@ -186,9 +183,8 @@
         for e in range(C):
             if d or e:
                 keys_copy(e, d).start()
-    for n in range(1, 4):
-        for d in range(1, Z):
-            z_copy(n, d).start()
+    for d in range(1, Z):
+        z_copy(1, d).start()
     tab_k[y * SHARE + c * Z + z] = k[at(c, ROWS), at(z, HEAD_SIZE)]
     vz[z] = v[:, at(z, HEAD_SIZE)]
     own_q = pltpu.make_async_copy(q.at[:, at(z, WIDE)], qh.at[z], own_sem.at[3])
@@ -268,7 +264,8 @@
             @pl.loop(first, first + count)
             def _(i):
                 for j in range(OTHERS):
-                    rows = tab[sel[1 + j, y * SHARE + to * Z + i]]
+                    block = sel[1 + j, y * SHARE + to * Z + i]
+                    rows = jnp.where(block < (y + 1) * SHARE, tab[block], 0.0).astype(tab.dtype)
                     if d:
                         out[d, i * OTHERS + j] = rows
                     else:
@@ -301,6 +298,9 @@
         ring_first(0)
         ring_next(0, 1)
 
+    for n in (2, 3):
+        for d in range(1, Z):
+            z_copy(n, d).start()
     for d in range(1, C):
         s_copy(0, d).start()
     kz[:, at(c, ROWS)] = tab_k[mine]

time: 163 us -> 162 us (level)
  no operation moved by 1% of the time
where the time goes in v6:
time: 162 us
  Pallas kernels  161 us (99%)
    pallas_call x1, Pallas kernels, whole(): pl.pallas_call(whole_kernel, out_shape=(jax.ShapeDtypeStruct((Z * BLOCK_T...  159 us

profile of v6, /device:TPU:1, one launch (start us, length us, event | category | flops | bytes accessed | tf_op | source)
XLA Modules:
  0.0 161.7 jit_solution(9299323229888132010)
XLA Ops:
  0.6 158.5 %whole.1 = (bf16[1024,512]{1,0:T(8,128)(2,1)}, bf16[8,128,128]{2,1,0:T(8,128)(2,1)}, bf16[8,128,128]{2,1,0:T(8,128)(2,1)}) custom-call(s32[8,512]{1,0:T(8,128)} %bitcast.5, s32[8,512]{1,0:T(8,128)} %bitcast.6, bf16[128,1024]{1,0:T(8,128)(2,1)} %k.1, bf16[128,1024]{1,0:T(8,128)(2,1)} %v.1, bf16[128,4096]{1,0:T(8,128)(2,1)} %q.1, bf16[128,4096]{1,0:T(8,128)(2,1)} %g.1), custom_call_target="tpu_custom_call" | custom-call | tf_op jit(solution)/shard_map/whole/pallas_call | solution.py:543
  159.2 2.5 %finish.1 = (bf16[1024,512]{1,0:T(8,128)(2,1)}, bf16[8,128,128]{2,1,0:T(8,128)(2,1)}, bf16[8,128,128]{2,1,0:T(8,128)(2,1)}) custom-call(bf16[1024,512]{1,0:T(8,128)(2,1)} %get-tuple-element.9.dq, bf16[8,128,128]{2,1,0:T(8,128)(2,1)} %get-tuple-element.10.dk, bf16[8,128,128]{2,1,0:T(8,128)(2,1)} %get-tuple-element.11.dv), custom_call_target="tpu_custom_call" | custom-call | tf_op jit(solution)/shard_map/finish/pallas_call | solution.py:591
